TPU v7x, 32 devices: a whole 2x2x4 slice. The times are simulated.
32 devices in a mesh: ctx: 16 (over z, y, core), head: 2 (over x).
Axes of the slice: x: 2, y: 2, z: 4, core: 2. Of those that a mesh axis runs over, the one named last changes fastest.
Arguments:
- teacher_q: bfloat16 [2, 1024, 8192], P(None, 'ctx'), may hold values from -48 to 48
- teacher_k: bfloat16 [2, 1024, 1024], P(None, 'ctx'), may hold values from -48 to 48
- student_in: bfloat16 [2, 1024, 2048], P(None, 'ctx'), may hold values from -56 to 56
- w_query: bfloat16 [2048, 2048], P('ctx'), may hold values from -0.125 to 0.125
- w_key: bfloat16 [2048, 2048], P('ctx'), may hold values from -0.125 to 0.125
Outputs:
- grad_query: float32 [2048, 2048], P('ctx')
- grad_key: float32 [2048, 2048], P('ctx')
All inputs are finite; a program needn't handle non-finite values.
Results may differ from a plain program's by a relative error of at most 0.01.
Values may be sent and summed in bfloat16 or wider, within the bound.
No kernel may reach another device: no remote copies, remote signals or barrier semaphores. Data moves between devices by JAX's collectives and lax.ppermute only.
A program may use at most 64 MiB of HBM per device.

v0:
```python
import functools
import math

import jax
import jax.numpy as jnp
from jax import lax
from jax.experimental import pallas as pl
from jax.experimental.pallas import tpu as pltpu
from jax.sharding import PartitionSpec as P

DTQ = 8192
DTK = 1024
DS = 2048
HEADS = 64
LOG2E = 1.4426950408889634
SPREAD = 80.0


def dot(a, b, ca, cb):
    return lax.dot_general(a, b, (((ca,), (cb,)), ((), ())), preferred_element_type=jnp.float32)


def turned(number, count):
    return sum(((number >> bit) & 1) * (count >> (bit + 1)) for bit in range(count.bit_length() - 1))


def rows_in(index, block):
    return pl.ds(index * block, block)


def masked(value, head, width):
    lane = lax.broadcasted_iota(jnp.int32, value.shape, 1)
    keep = (lane >= head * width) & (lane < (head + 1) * width)
    return jnp.where(keep, value, jnp.zeros_like(value))


def norms(ref, width, chosen):
    first, last = chosen[0], chosen[-1] + 1
    if (first * width) % 128 == 0 and (last * width) % 128 == 0:
        value = ref[:, first * width : last * width].astype(jnp.float32)
    else:
        value, first = ref[...].astype(jnp.float32), 0
    square = (value * value).astype(jnp.bfloat16)
    column = lax.broadcasted_iota(jnp.int32, (square.shape[1], 128), 0) + first * width
    lane = lax.broadcasted_iota(jnp.int32, (square.shape[1], 128), 1)
    member = ((column >= lane * width) & (column < (lane + 1) * width)).astype(jnp.bfloat16)
    total = dot(square, member, 1, 0)
    factor = LOG2E / math.sqrt(width)
    high = jnp.max(total, axis=0, keepdims=True) * (factor * (1 + 2**-6))
    low = jnp.min(total, axis=0, keepdims=True) * (factor * (1 - 2**-6))
    lane = lax.broadcasted_iota(jnp.int32, (1, 128), 1)
    gap = jnp.where((lane >= chosen[0]) & (lane < last), high - low, 0.0)
    return high, jnp.max(gap)


def gradients(t_ref, s_ref, et_ref, es_ref, g_ref, gt_ref, *, heads, chosen, teach, block):
    rows, feats = s_ref.shape
    blocks = rows // block
    stud = feats // heads
    factors = tuple(LOG2E / math.sqrt(width) for width in (teach, stud))
    aligned = teach % 128 == 0

    def teacher(index, head):
        if aligned:
            part = t_ref.at[:, pl.ds(head * teach, teach)]
            return part[rows_in(index, block), :], part[...]
        return masked(t_ref[rows_in(index, block), :], head, teach), t_ref[...]

    def student(index, head):
        return masked(s_ref[rows_in(index, block), :], head, stud), s_ref[...]

    g_ref[...] = jnp.zeros_like(g_ref)
    gt_ref[...] = jnp.zeros_like(gt_ref)
    top_t, gap_t = norms(t_ref, teach, chosen)
    top_s, gap_s = norms(s_ref, stud, chosen)
    safe = jnp.maximum(gap_t, gap_s) < SPREAD

    @pl.when(safe)
    def _():
        flipped = s_ref[...].T
        for head in chosen:
            pick = slice(head, head + 1)
            sums = []
            for own, e_ref, factor, top in (
                (teacher, et_ref, factors[0], top_t[:, pick]),
                (student, es_ref, factors[1], top_s[:, pick]),
            ):
                down = [jnp.zeros((1, block), jnp.float32) for _ in range(blocks)]
                along = []
                for index in range(blocks):
                    left, right = own(index, head)
                    lo = index * block
                    e = jnp.exp2(dot(left, right[lo:], 1, 1) * factor - top)
                    e_ref[rows_in(index, block), lo:] = e
                    for other in range(index, blocks):
                        part = e[:, other * block - lo : (other + 1) * block - lo]
                        down[other] = down[other] + jnp.sum(part, axis=0, keepdims=True)
                    width = math.gcd(block, 128)
                    parts = [e[:, at : at + width] for at in range(block, e.shape[1], width)]
                    along.append(sum(parts) if parts else jnp.zeros((block, width), jnp.float32))
                along = jnp.sum(jnp.concatenate(along, axis=0).T, axis=0, keepdims=True)
                sums.append(jnp.concatenate(down, axis=1) + along)
            across = [1.0 / total for total in sums]
            down = [jnp.broadcast_to(a, (128, rows)).T[:, :1] for a in across]
            right = masked(s_ref[...], head, stud)
            for index in range(blocks):
                lo = index * block
                here = rows_in(index, block)
                h = es_ref[here, lo:] * (down[1][lo : lo + block] + across[1][:, lo:])
                h = h - et_ref[here, lo:] * (down[0][lo : lo + block] + across[0][:, lo:])
                h = h.astype(jnp.bfloat16)
                g_ref[here, :] += dot(h, right[lo:], 1, 0)
                if index < blocks - 1:
                    feats_here = slice(head * stud, (head + 1) * stud)
                    left = flipped[feats_here, lo : lo + block]
                    gt_ref[feats_here, lo + block :] += dot(left, h[:, block:], 1, 0)

    @pl.when(jnp.logical_not(safe))
    def _():
        for head in chosen:

            def step(index, carry):
                here = rows_in(index, block)
                probs = []
                for k, own in enumerate((teacher, student)):
                    left, right = own(index, head)
                    score = dot(left, right, 1, 1) * (factors[k] / LOG2E)
                    e = jnp.exp(score - jnp.max(score, axis=1, keepdims=True))
                    probs.append(e / jnp.sum(e, axis=1, keepdims=True))
                difference = probs[1] - probs[0]
                right = masked(s_ref[...], head, stud)
                g_ref[here, :] += dot(difference.astype(jnp.bfloat16), right, 1, 0)
                left = masked(s_ref[here, :], head, stud)
                g_ref[...] += dot(difference.T.astype(jnp.bfloat16), left, 1, 0)
                return carry

            lax.fori_loop(0, blocks, step, 0)


def weight_grad(g_ref, gt_ref, x_ref, o_ref, first, stud):
    grad = ((g_ref[...].T + gt_ref[...]) * (1.0 / math.sqrt(stud))).astype(jnp.bfloat16)
    grad = grad[first : first + o_ref.shape[0]]
    columns = math.gcd(x_ref.shape[1], 512)
    for lo in range(0, x_ref.shape[1], columns):
        part = pl.ds(lo, columns)
        o_ref[:, part] = dot(grad, x_ref[:, part], 1, 0).astype(jnp.bfloat16)


def split_kernel(t_ref, o_ref, sems):
    own = t_ref.at[lax.axis_index("head")]
    places, _, width = o_ref.shape
    copies = [
        pltpu.make_async_copy(own.at[:, pl.ds(place * width, width)], o_ref.at[place], sems.at[place])
        for place in range(places)
    ]
    for copy in copies:
        copy.start()
    for copy in copies:
        copy.wait()


def split(t, places):
    return pl.pallas_call(
        split_kernel,
        out_shape=jax.ShapeDtypeStruct((places, t.shape[1], t.shape[2] // places), t.dtype),
        in_specs=[HBM],
        out_specs=VMEM,
        scratch_shapes=[pltpu.SemaphoreType.DMA((places,))],
        name="split",
    )(t)


def key_kernel(*refs, spots, heads, teach, block):
    count = len(spots)
    pieces, refs = refs[:count], refs[count:]
    wq_hbm, wk_hbm, own_ref, twin_ref, x_hbm, sq_ref, o_ref, *refs = refs
    x_ref, wq_ref, wk_ref, sk_ref, t_ref, et_ref, es_ref, g_ref, gt_ref, sems = refs
    places = lax.axis_size("ctx")
    where = lax.axis_index("ctx")
    levels = places // 4
    rows = x_ref.shape[0]
    tokens = rows // places
    chip, core = where // 2, where % 2
    level, side = chip // 2, chip % 2
    position = jnp.where(side == 0, level, 2 * levels - 1 - level)
    copies = []
    for number, (piece, (step, twin, offset)) in enumerate(zip(pieces, spots)):
        other = (position + step + 2 * levels) % (2 * levels)
        other = jnp.where(other < levels, 2 * other, 2 * (2 * levels - 1 - other) + 1)
        row = pl.multiple_of((other * 2 + (core + twin) % 2) * tokens + offset, piece.shape[0])
        target = x_ref.at[pl.ds(row, piece.shape[0]), :]
        copies.append(pltpu.make_async_copy(piece, target, sems.at[number]))
    for number, (source, target) in enumerate(((wq_hbm, wq_ref), (wk_hbm, wk_ref))):
        copies.append(pltpu.make_async_copy(source, target, sems.at[count + number]))
    for copy in copies:
        copy.start()
    chips = places // 2
    for twin, ref in enumerate((own_ref, twin_ref)):
        part = ref[...].astype(jnp.float32)
        part = jnp.where(core == 1, pltpu.roll(part, part.shape[1] // 2, 1), part).astype(jnp.bfloat16)
        for number in range(chips):
            row = ((chip ^ turned(number, chips)) * 2 + (core + twin) % 2) * tokens
            here = pl.ds(pl.multiple_of(row, tokens), tokens)
            t_ref[here, :] = part[number * tokens : (number + 1) * tokens]
    for copy in copies:
        copy.wait()
    leave = pltpu.make_async_copy(x_ref, x_hbm, sems.at[0])
    leave.start()
    for index in range(rows // block):
        here = rows_in(index, block)
        sq_ref[here, :] = dot(x_ref[here, :], wq_ref[...], 1, 1).astype(jnp.bfloat16)
        sk_ref[here, :] = dot(x_ref[here, :], wk_ref[...], 1, 1).astype(jnp.bfloat16)
    gradients(
        t_ref,
        sk_ref,
        et_ref,
        es_ref,
        g_ref,
        gt_ref,
        heads=heads,
        chosen=range(heads),
        teach=teach,
        block=block,
    )
    weight_grad(g_ref, gt_ref, x_ref, o_ref, 0, wk_ref.shape[0] // heads)
    leave.wait()


def query_kernel(
    x_hbm, s_ref, t_ref, o_ref, x_ref, et_ref, es_ref, g_ref, gt_ref, sem, *, heads, chosen, block
):
    fetch = pltpu.make_async_copy(x_hbm, x_ref, sem)
    fetch.start()
    stud = s_ref.shape[1] // heads
    gradients(
        t_ref,
        s_ref,
        et_ref,
        es_ref,
        g_ref,
        gt_ref,
        heads=heads,
        chosen=chosen,
        teach=t_ref.shape[1] // heads,
        block=block,
    )
    fetch.wait()
    weight_grad(g_ref, gt_ref, x_ref, o_ref, chosen[0] * stud, stud)


def cost(rows, heads):
    return pl.CostEstimate(
        flops=2 * rows * rows * 256 * 3 * heads,
        bytes_accessed=4 * rows * rows,
        transcendentals=2 * rows * rows * heads,
    )


VMEM = pl.BlockSpec(memory_space=pltpu.VMEM)
HBM = pl.BlockSpec(memory_space=pltpu.HBM)
LIMIT = pltpu.CompilerParams(vmem_limit_bytes=20 * 2**20)


def in_hbm(*values):
    return [pltpu.with_memory_space_constraint(value, pltpu.HBM) for value in values]


def key_part(pieces, spots, w_query, w_key, own, twin, heads):
    feats, width = w_key.shape
    rows = 2 * own.shape[0]
    score = pltpu.VMEM((rows, rows), jnp.float32)
    return pl.pallas_call(
        functools.partial(
            key_kernel,
            spots=tuple(spots),
            heads=heads,
            teach=own.shape[1] // 2 // heads,
            block=math.gcd(rows, 256),
        ),
        out_shape=(
            pltpu.HBM((rows, width), jnp.bfloat16),
            pltpu.VMEM((rows, feats), jnp.bfloat16),
            jax.ShapeDtypeStruct((feats, width), jnp.bfloat16),
        ),
        in_specs=[HBM] * (len(pieces) + 2) + [VMEM] * 2,
        out_specs=(HBM, VMEM, VMEM),
        scratch_shapes=[
            pltpu.VMEM((rows, width), jnp.bfloat16),
            pltpu.VMEM(w_query.shape, jnp.bfloat16),
            pltpu.VMEM(w_key.shape, jnp.bfloat16),
            pltpu.VMEM((rows, feats), jnp.bfloat16),
            pltpu.VMEM((rows, own.shape[1]), jnp.bfloat16),
            score,
            score,
            pltpu.VMEM((rows, feats), jnp.float32),
            pltpu.VMEM((feats, rows), jnp.float32),
            pltpu.SemaphoreType.DMA((len(pieces) + 2,)),
        ],
        compiler_params=LIMIT,
        cost_estimate=cost(rows, heads),
        name="key_type",
    )(*in_hbm(*pieces, w_query, w_key), own, twin)


def query_part(x, s, t, heads, chosen):
    rows, width = x.shape
    stud = s.shape[1] // heads
    score = pltpu.VMEM((rows, rows), jnp.float32)
    return pl.pallas_call(
        functools.partial(query_kernel, heads=heads, chosen=chosen, block=math.gcd(rows, 256)),
        out_shape=jax.ShapeDtypeStruct((len(chosen) * stud, width), jnp.bfloat16),
        in_specs=[HBM, VMEM, VMEM],
        out_specs=VMEM,
        scratch_shapes=[
            pltpu.VMEM(x.shape, jnp.bfloat16),
            score,
            score,
            pltpu.VMEM(s.shape, jnp.float32),
            pltpu.VMEM(s.shape[::-1], jnp.float32),
            pltpu.SemaphoreType.DMA,
        ],
        compiler_params=LIMIT,
        cost_estimate=cost(rows, len(chosen)),
        name="query_type",
    )(*in_hbm(x), pltpu.with_memory_space_constraint(s, pltpu.VMEM), t)


def by_sequence(teacher_q, teacher_k, student_in, w_query, w_key):
    places = lax.axis_size("ctx")
    levels = places // 4
    heads = HEADS // places
    index = lax.axis_index("head")
    own_k, own_x = (lax.dynamic_index_in_dim(value, index, 0, False) for value in (teacher_k, student_in))
    tokens = own_x.shape[0]

    ring = [2 * k for k in range(levels)] + [2 * k + 1 for k in reversed(range(levels))]
    count = len(ring)
    forward, backward, twin = [], [], []
    for position in range(count):
        for core in range(2):
            here = ring[position] * 2 + core
            forward.append((here, ring[(position + 1) % count] * 2 + core))
            backward.append((here, ring[position - 1] * 2 + core))
            twin.append((here, here ^ 1))

    pieces, spots = [], []

    def keep(value, step, offset=0):
        pieces.extend((value, lax.ppermute(value, "ctx", twin)))
        spots.extend(((step, 0, offset), (step, 1, offset)))

    chip = lax.axis_index("ctx") // 2

    def halve(keys, bit):
        width = keys.shape[1] // 2
        mine = jnp.where(chip & bit, width, 0)
        stay = lax.dynamic_slice_in_dim(keys, mine, width, 1)
        leave = lax.dynamic_slice_in_dim(keys, width - mine, width, 1)
        got = lax.ppermute(leave, "ctx", [(i, i ^ (2 * bit)) for i in range(places)])
        return stay, got

    half = tokens // 2
    bits = [1 << bit for bit in reversed(range(count.bit_length() - 1))]
    pair = halve(own_k, bits.pop(0))
    parts = split(teacher_q, places)
    keep(own_x, 0)
    ahead = behind = own_x
    for step in range(1, count // 2):
        ahead = lax.ppermute(ahead, "ctx", forward)
        behind = lax.ppermute(behind, "ctx", backward)
        keep(ahead, -step)
        keep(behind, step)
        if bits:
            ahead, behind, pair = lax.optimization_barrier((ahead, behind, pair))
            pair = halve(jnp.concatenate(pair), bits.pop(0))
    ahead = lax.ppermute(ahead[:half], "ctx", forward)
    behind = lax.ppermute(behind[half:], "ctx", backward)
    keep(ahead, -(count // 2))
    keep(behind, count // 2, half)
    for bit in bits:
        pair = halve(jnp.concatenate(pair), bit)
    keys = jnp.concatenate(pair)
    twin_keys = lax.ppermute(keys, "ctx", twin)

    parts, _, keys = lax.optimization_barrier((parts, (ahead, behind), keys))
    tq = lax.all_to_all(parts, "ctx", 0, 0, tiled=True).reshape(places * tokens, parts.shape[2])

    x, s, part_k = key_part(pieces, spots, w_query, w_key, keys, twin_keys, heads)

    def swap(part):
        return lax.ppermute(part, "head", [(0, 1), (1, 0)])

    def both(part, other):
        return part.astype(jnp.float32) + other.astype(jnp.float32)

    first, last = (tuple(range(lo, lo + heads // 2)) for lo in (0, heads // 2))
    other_k = swap(part_k)
    part = query_part(x, s, tq, heads, first)
    other = swap(part)
    s, part = lax.optimization_barrier((s, part))
    part_last = query_part(x, s, tq, heads, last)
    other_last = swap(part_last)
    other_k, other, part_last = lax.optimization_barrier((other_k, other, part_last))
    grad_q = jnp.pad(both(part, other), ((0, part_last.shape[0]), (0, 0)))
    grad_q = lax.dynamic_update_slice(grad_q, both(part_last, other_last), (part.shape[0], 0))
    return grad_q, both(part_k, other_k)


def score_tile(local_part, key_part, offset, tile_width, head_width):
    key_tile = lax.dynamic_slice_in_dim(key_part, offset, tile_width, 2)
    product = lax.dot_general(
        local_part, key_tile, (((1,), (1,)), ((0,), (0,))), preferred_element_type=jnp.float32
    )
    return product / math.sqrt(head_width)


def by_rows(teacher_q, teacher_k, student_in, w_query, w_key):
    query_width = DTQ // HEADS
    key_width = DTK // HEADS
    stud_width = DS // HEADS
    batch_count = teacher_q.shape[0]
    share = teacher_q.shape[1] // lax.axis_size("head")
    first = lax.axis_index("head") * share
    own_query = lax.dynamic_slice_in_dim(teacher_q, first, share, 1)
    own_key = lax.dynamic_slice_in_dim(teacher_k, first, share, 1)
    own_input = lax.dynamic_slice_in_dim(student_in, first, share, 1)
    teach_query, teach_key = (
        lax.all_to_all(
            own_query.transpose(2, 0, 1), "ctx", split_axis=0, concat_axis=2, tiled=True
        ),
        lax.all_to_all(own_key.transpose(2, 0, 1), "ctx", split_axis=0, concat_axis=2, tiled=True),
    )
    student_rows = lax.all_gather(own_input, "ctx", axis=1, tiled=True)
    row_count = student_rows.shape[1]
    across = (((1,), (2,)), ((), ()))
    stud_query = lax.dot_general(
        w_query, student_rows, across, preferred_element_type=jnp.float32
    ).astype(jnp.bfloat16)
    stud_key = lax.dot_general(
        w_key, student_rows, across, preferred_element_type=jnp.float32
    ).astype(jnp.bfloat16)
    heads_here = stud_query.shape[0] // stud_width
    gathered_all = (
        lax.all_gather(teach_query, "head", axis=2, tiled=True),
        lax.all_gather(teach_key, "head", axis=2, tiled=True),
        lax.all_gather(stud_query, "head", axis=2, tiled=True),
        lax.all_gather(stud_key, "head", axis=2, tiled=True),
    )
    own_all = (teach_query, teach_key, stud_query, stud_key)
    key_count = gathered_all[0].shape[2]
    widths = (query_width, key_width, stud_width, stud_width)
    tile_width = math.gcd(key_count, 512)
    tile_count = key_count // tile_width
    tiles = jnp.arange(tile_count)
    batched = (((2,), (2,)), ((0,), (0,)))
    weight_query = jnp.zeros((heads_here * stud_width, w_query.shape[1]), jnp.float32)
    weight_key = jnp.zeros((heads_here * stud_width, w_key.shape[1]), jnp.float32)
    for index in range(batch_count):
        local_parts = tuple(
            (
                own_all[member][:, index, :].reshape(heads_here, widths[member], row_count)
                for member in range(4)
            )
        )
        key_parts = tuple(
            (
                gathered_all[member][:, index, :].reshape(heads_here, widths[member], key_count)
                for member in range(4)
            )
        )

        def stat_step(state_now, tile_index):
            offset = tile_index * tile_width
            updated = []
            for member in range(4):
                running_max, running_sum = state_now[member]
                scores = score_tile(
                    local_parts[member], key_parts[member], offset, tile_width, widths[member]
                )
                new_max = jnp.maximum(running_max, jnp.max(scores, axis=2))
                running_sum = running_sum * jnp.exp(running_max - new_max) + jnp.sum(
                    jnp.exp(scores - new_max[:, :, None]), axis=2
                )
                updated.append((new_max, running_sum))
            return (tuple(updated), None)

        start_stats = tuple(
            (
                (
                    jnp.full((heads_here, row_count), -jnp.inf, jnp.float32),
                    jnp.zeros((heads_here, row_count), jnp.float32),
                )
                for member in range(4)
            )
        )
        final_stats, unused = lax.scan(stat_step, start_stats, tiles)
        log_totals = tuple(
            (final_stats[member][0] + jnp.log(final_stats[member][1]) for member in range(4))
        )
        zero_terms = jnp.zeros((heads_here, stud_width, row_count), jnp.float32)

        def grad_step(state_now, tile_index):
            offset = tile_index * tile_width
            scores = [
                score_tile(
                    local_parts[member], key_parts[member], offset, tile_width, widths[member]
                )
                for member in range(4)
            ]
            row_probs = [
                jnp.exp(scores[member] - log_totals[member][:, :, None]) for member in range(4)
            ]
            differences = (
                (row_probs[2] - row_probs[0]).astype(jnp.bfloat16),
                (row_probs[3] - row_probs[1]).astype(jnp.bfloat16),
            )
            key_tiles = (
                lax.dynamic_slice_in_dim(key_parts[2], offset, tile_width, 2),
                lax.dynamic_slice_in_dim(key_parts[3], offset, tile_width, 2),
            )
            row_terms = tuple(
                (
                    state_now[member]
                    + lax.dot_general(
                        key_tiles[member],
                        differences[member],
                        batched,
                        preferred_element_type=jnp.float32,
                    )
                    for member in range(2)
                )
            )
            contrib = tuple(
                (
                    lax.dot_general(
                        local_parts[2 + member],
                        differences[member],
                        (((2,), (1,)), ((0,), (0,))),
                        preferred_element_type=jnp.float32,
                    )
                    for member in range(2)
                )
            )
            return (row_terms, contrib)

        sums, pieces = lax.scan(grad_step, (zero_terms, zero_terms), tiles)
        row_query, row_key = sums
        spread = tuple(
            (
                pieces[member].transpose(1, 2, 0, 3).reshape(heads_here, stud_width, key_count)
                for member in range(2)
            )
        )
        col_query, col_key = (
            lax.psum_scatter(
                spread[0].astype(jnp.bfloat16), "head", scatter_dimension=2, tiled=True
            ).astype(jnp.float32),
            lax.psum_scatter(
                spread[1].astype(jnp.bfloat16), "head", scatter_dimension=2, tiled=True
            ).astype(jnp.float32),
        )
        query_grad = (
            ((row_query + col_query) / math.sqrt(stud_width))
            .astype(jnp.bfloat16)
            .reshape(heads_here * stud_width, row_count)
        )
        key_grad = (
            ((row_key + col_key) / math.sqrt(stud_width))
            .astype(jnp.bfloat16)
            .reshape(heads_here * stud_width, row_count)
        )
        weight_query = weight_query + lax.dot_general(
            query_grad,
            student_rows[index],
            (((1,), (0,)), ((), ())),
            preferred_element_type=jnp.float32,
        )
        weight_key = weight_key + lax.dot_general(
            key_grad,
            student_rows[index],
            (((1,), (0,)), ((), ())),
            preferred_element_type=jnp.float32,
        )
    grad_query, grad_key = (
        lax.psum(weight_query.astype(jnp.bfloat16), "head").astype(jnp.float32),
        lax.psum(weight_key.astype(jnp.bfloat16), "head").astype(jnp.float32),
    )
    return (grad_query, grad_key)


def solution(mesh):
    placed = (
        P(None, "ctx", None),
        P(None, "ctx", None),
        P(None, "ctx", None),
        P("ctx", None),
        P("ctx", None),
    )
    places = mesh.shape["ctx"]

    def on_device(*args):
        batch, tokens, _ = args[0].shape
        even = places in (4, 8, 16, 32) and tokens % 32 == 0
        if even and batch == mesh.shape["head"] == 2 and tokens * places <= 1024:
            return by_sequence(*args)
        return by_rows(*args)

    return jax.shard_map(
        on_device,
        mesh=mesh,
        in_specs=placed,
        out_specs=(P("ctx", None), P("ctx", None)),
        check_vma=False,
    )
```

profile of v0, /device:TPU:0, one launch (start us, length us, event | category | flops | bytes accessed | tf_op | source)
XLA Modules:
  0.0 112.3 jit_solution(17325183017646534590)
XLA Ops:
  0.6 1.0 copy-done
  1.7 3.0 %collective-permute-start.3 = (bf16[64,2048]{1,0:T(8,128)(2,1)S(1)}, bf16[64,2048]{1,0:T(8,128)(2,1)S(1)}, u32[]{:S(2)}, u32[]{:S(2)}) collective-permute-start(bf16[64,2048]{1,0:T(8,128)(2,1)S(1)} %dynamic-slice_bitcast_fusion.refs_0_), channel_id=1, source_target_pairs={{0,4},{2,6},{8,0},{10,2},{16,8},{18,10},{24,16},{26,18},{28,24},{3... | collective-permute-start | bytes 786440 | tf_op jit(solution)/shard_map/ppermute | solution.py:370
  4.7 0.1 collective-permute-start.1
  4.9 1.1 dynamic-slice_bitcast_fusion.1
  5.9 3.0 %collective-permute-start.5 = (bf16[64,512]{1,0:T(8,128)(2,1)S(1)}, bf16[64,512]{1,0:T(8,128)(2,1)S(1)}, u32[]{:S(2)}, u32[]{:S(2)}) collective-permute-start(bf16[64,512]{1,0:T(8,128)(2,1)S(1)} %get-tuple-element.38), channel_id=1, source_target_pairs={{0,16},{2,18},{4,20},{6,22},{8,24},{10,26},{12,28},{14,30},{16,0},... | collective-permute-start | bytes 196616 | tf_op jit(solution)/shard_map/ppermute | solution.py:359
  8.9 6.2 %collective-permute-done.5 = bf16[64,512]{1,0:T(8,128)(2,1)S(1)} collective-permute-done((bf16[64,512]{1,0:T(8,128)(2,1)S(1)}, bf16[64,512]{1,0:T(8,128)(2,1)S(1)}, u32[]{:S(2)}, u32[]{:S(2)}) %collective-permute-start.5) | collective-permute-done | bytes 65568 | tf_op jit(solution)/shard_map/ppermute | solution.py:359
  15.1 0.3 collective-permute-start.6
  15.4 2.6 %collective-permute-start.8 = (bf16[64,2048]{1,0:T(8,128)(2,1)S(1)}, bf16[64,2048]{1,0:T(8,128)(2,1)S(1)}, u32[]{:S(2)}, u32[]{:S(2)}) collective-permute-start(bf16[64,2048]{1,0:T(8,128)(2,1)S(1)} %collective-permute-done.3.refs_4_), channel_id=1, source_target_pairs={{0,4},{2,6},{8,0},{10,2},{16,8},{18,10},{24,16},{26,18},{28,24},{3... | collective-permute-start | bytes 786440 | tf_op jit(solution)/shard_map/ppermute | solution.py:370
  18.2 5.2 %collective-permute-done.10 = bf16[128,256]{1,0:T(8,128)(2,1)S(1)} collective-permute-done((bf16[128,256]{1,0:T(8,128)(2,1)S(1)}, bf16[128,256]{1,0:T(8,128)(2,1)S(1)}, u32[]{:S(2)}, u32[]{:S(2)}) %collective-permute-start.10) | collective-permute-done | bytes 65568 | tf_op jit(solution)/shard_map/ppermute | solution.py:359
  23.4 0.3 collective-permute-start.11
  23.7 2.3 %collective-permute-start.13 = (bf16[64,2048]{1,0:T(8,128)(2,1)S(1)}, bf16[64,2048]{1,0:T(8,128)(2,1)S(1)}, u32[]{:S(2)}, u32[]{:S(2)}) collective-permute-start(bf16[64,2048]{1,0:T(8,128)(2,1)S(1)} %collective-permute-done.8.refs_8_), channel_id=1, source_target_pairs={{0,4},{2,6},{8,0},{10,2},{16,8},{18,10},{24,16},{26,18},{28,24},{3... | collective-permute-start | bytes 786440 | tf_op jit(solution)/shard_map/ppermute | solution.py:370
  26.0 2.3 %collective-permute-start.19 = (bf16[256,128]{1,0:T(8,128)(2,1)S(1)}, bf16[256,128]{1,0:T(8,128)(2,1)S(1)}, u32[]{:S(2)}, u32[]{:S(2)}) collective-permute-start(bf16[256,128]{1,0:T(8,128)(2,1)S(1)} %get-tuple-element.41), channel_id=1, source_target_pairs={{0,4},{2,6},{4,0},{6,2},{8,12},{10,14},{12,8},{14,10},{16,20},{18,... | collective-permute-start | bytes 196616 | tf_op jit(solution)/shard_map/ppermute | solution.py:359
  28.3 3.4 %collective-permute-done.11.refs_10_ = bf16[64,2048]{1,0:T(8,128)(2,1)S(1)} collective-permute-done((bf16[64,2048]{1,0:T(8,128)(2,1)S(1)}, bf16[64,2048]{1,0:T(8,128)(2,1)S(1)}, u32[]{:S(2)}, u32[]{:S(2)}) %collective-permute-start.11) | collective-permute-done | bytes 262176 | tf_op jit(solution)/shard_map/ppermute | solution.py:369
  31.7 0.4 collective-permute-start.15
  32.1 0.2 collective-permute-done.13.refs_12_
  32.3 1.8 %collective-permute-start.17 = (bf16[32,2048]{1,0:T(8,128)(2,1)S(1)}, bf16[32,2048]{1,0:T(8,128)(2,1)S(1)}, u32[]{:S(2)}, u32[]{:S(2)}) collective-permute-start(bf16[32,2048]{1,0:T(8,128)(2,1)S(1)} %slice.9), channel_id=1, source_target_pairs={{0,4},{2,6},{8,0},{10,2},{16,8},{18,10},{24,16},{26,18},{28,24},{3... | collective-permute-start | bytes 393224 | tf_op jit(solution)/shard_map/ppermute | solution.py:377
  34.1 2.3 %split.1 = bf16[16,64,512]{2,1,0:T(8,128)(2,1)} custom-call(bf16[2,64,8192]{2,1,0:T(8,128)(2,1)} %t_ref.1), custom_call_target="tpu_custom_call" | custom-call | tf_op jit(solution)/shard_map/split/pallas_call | solution.py:163
  36.5 0.5 collective-permute-done.15.refs_14_
  36.9 0.6 collective-permute-done.17.refs_16_
  37.6 0.6 copy-done.16
  38.2 5.3 %all-to-all-start = ((bf16[16,64,512]{2,1,0:T(8,128)(2,1)}), bf16[16,64,512]{2,1,0:T(8,128)(2,1)S(1)}, u32[]{:S(2)}, u32[]{:S(2)}) async-start(bf16[16,64,512]{2,1,0:T(8,128)(2,1)} %split.1), calls=%async_computation | async-start | bytes 2097152 | tf_op jit(solution)/shard_map/all_to_all | solution.py:386
  43.5 0.4 collective-permute-start
  43.9 0.2 collective-permute-start.4
  44.1 0.3 collective-permute-start.2
  44.4 0.2 collective-permute-start.7
  44.6 0.3 collective-permute-start.20
  44.9 0.2 collective-permute-done.refs_1_
  45.1 0.3 collective-permute-start.9
  45.5 0.3 collective-permute-start.12
  45.9 0.3 collective-permute-start.14
  46.2 0.2 collective-permute-done.20.refs_21_
  46.4 0.3 collective-permute-start.16
  46.8 0.2 collective-permute-start.18
  46.9 1.0 collective-permute-done.16.refs_15_
  48.0 0.3 collective-permute-done.18.refs_17_
  48.5 0.2 copy-done.17
  48.6 0.3 copy-done.18
  49.0 0.1 copy-done.13
  49.1 0.7 copy-done.14
  49.8 27.1 %key_type.1 = (bf16[1024,2048]{1,0:T(8,128)(2,1)}, bf16[1024,128]{1,0:T(8,128)(2,1)S(1)}, bf16[128,2048]{1,0:T(8,128)(2,1)S(1)}) custom-call(bf16[64,2048]{1,0:T(8,128)(2,1)} %copy-done.1, bf16[64,2048]{1,0:T(8,128)(2,1)} %copy-done.8, bf16[64,2048]{1,0:T(8,128)(2,1)} %copy-done.5, bf16[64,2048]{1,0:T(8,128)(2,1)} %copy-done.10, bf16[64,2048]{1,0:T(8,128)(2,1)} %copy-done.4, ...), custom_call_target="tpu_custom_call" | custom-call | flops 6442450944 | bytes 4194304 | tf_op jit(solution)/shard_map/key_type/pallas_call | solution.py:272
  76.9 1.6 %collective-permute-start.21 = (bf16[128,2048]{1,0:T(8,128)(2,1)S(1)}, bf16[128,2048]{1,0:T(8,128)(2,1)S(1)}, u32[]{:S(2)}, u32[]{:S(2)}) collective-permute-start(bf16[128,2048]{1,0:T(8,128)(2,1)S(1)} %get-tuple-element.33), channel_id=1, source_target_pairs={{0,1},{1,0},{2,3},{3,2},{4,5},{5,4},{6,7},{7,6},{8,9},{9,8},{10,11... | collective-permute-start | bytes 1572872 | tf_op jit(solution)/shard_map/ppermute | solution.py:391
  78.5 12.2 %query_type.2 = bf16[64,2048]{1,0:T(8,128)(2,1)S(1)} custom-call(bf16[1024,2048]{1,0:T(8,128)(2,1)} %get-tuple-element.30.x_hbm, bf16[1024,128]{1,0:T(8,128)(2,1)S(1)} %get-tuple-element.34.s_ref, bf16[1024,512]{1,0:T(8,128)(2,1)S(1)} %bitcast.7), custom_call_target="tpu_custom_call" | custom-call | flops 3221225472 | bytes 4194304 | tf_op jit(solution)/shard_map/query_type/pallas_call | solution.py:309
  90.7 0.6 collective-permute-start.22
  91.3 12.0 %query_type.3 = bf16[64,2048]{1,0:T(8,128)(2,1)S(1)} custom-call(bf16[1024,2048]{1,0:T(8,128)(2,1)} %get-tuple-element.30.x_hbm, bf16[1024,128]{1,0:T(8,128)(2,1)S(1)} %get-tuple-element.34.s_ref, bf16[1024,512]{1,0:T(8,128)(2,1)S(1)} %bitcast.8), custom_call_target="tpu_custom_call" | custom-call | flops 3221225472 | bytes 4194304 | tf_op jit(solution)/shard_map/query_type/pallas_call | solution.py:309
  103.3 1.6 %collective-permute-start.23 = (bf16[64,2048]{1,0:T(8,128)(2,1)S(1)}, bf16[64,2048]{1,0:T(8,128)(2,1)S(1)}, u32[]{:S(2)}, u32[]{:S(2)}) collective-permute-start(bf16[64,2048]{1,0:T(8,128)(2,1)S(1)} %query_type.3), channel_id=1, source_target_pairs={{0,1},{1,0},{2,3},{3,2},{4,5},{5,4},{6,7},{7,6},{8,9},{9,8},{10,11... | collective-permute-start | bytes 786440 | tf_op jit(solution)/shard_map/ppermute | solution.py:391
  104.9 1.1 convert_add_fusion
  106.0 5.1 %collective-permute-done.23 = bf16[64,2048]{1,0:T(8,128)(2,1)S(1)} collective-permute-done((bf16[64,2048]{1,0:T(8,128)(2,1)S(1)}, bf16[64,2048]{1,0:T(8,128)(2,1)S(1)}, u32[]{:S(2)}, u32[]{:S(2)}) %collective-permute-start.23) | collective-permute-done | bytes 262176 | tf_op jit(solution)/shard_map/ppermute | solution.py:391
  111.2 1.0 pad_maximum_fusion
  (59 shorter events, 0.4 us)
Async XLA Ops:
  0.6 1.0 copy-start
  1.7 46.7 %copy-start.1 = (bf16[64,2048]{1,0:T(8,128)(2,1)}, bf16[64,2048]{1,0:T(8,128)(2,1)S(1)}, u32[]{:S(2)}) copy-start(bf16[64,2048]{1,0:T(8,128)(2,1)S(1)} %dynamic-slice_bitcast_fusion.refs_0_) | copy-start | bytes 786436
  1.7 13.4 %collective-permute-start.3 = (bf16[64,2048]{1,0:T(8,128)(2,1)S(1)}, bf16[64,2048]{1,0:T(8,128)(2,1)S(1)}, u32[]{:S(2)}, u32[]{:S(2)}) collective-permute-start(bf16[64,2048]{1,0:T(8,128)(2,1)S(1)} %dynamic-slice_bitcast_fusion.refs_0_), channel_id=1, source_target_pairs={{0,4},{2,6},{8,0},{10,2},{16,8},{18,10},{24,16},{26,18},{28,24},{3... | collective-permute-start | bytes 786440 | tf_op jit(solution)/shard_map/ppermute | solution.py:370
  4.7 10.4 %collective-permute-start.1 = (bf16[64,2048]{1,0:T(8,128)(2,1)S(1)}, bf16[64,2048]{1,0:T(8,128)(2,1)S(1)}, u32[]{:S(2)}, u32[]{:S(2)}) collective-permute-start(bf16[64,2048]{1,0:T(8,128)(2,1)S(1)} %dynamic-slice_bitcast_fusion.refs_0_), channel_id=1, source_target_pairs={{0,8},{2,10},{8,16},{10,18},{16,24},{18,26},{24,28},{26,30},{28,20... | collective-permute-start | bytes 786440 | tf_op jit(solution)/shard_map/ppermute | solution.py:369
  5.9 9.1 %collective-permute-start.5 = (bf16[64,512]{1,0:T(8,128)(2,1)S(1)}, bf16[64,512]{1,0:T(8,128)(2,1)S(1)}, u32[]{:S(2)}, u32[]{:S(2)}) collective-permute-start(bf16[64,512]{1,0:T(8,128)(2,1)S(1)} %get-tuple-element.38), channel_id=1, source_target_pairs={{0,16},{2,18},{4,20},{6,22},{8,24},{10,26},{12,28},{14,30},{16,0},... | collective-permute-start | bytes 196616 | tf_op jit(solution)/shard_map/ppermute | solution.py:359
  15.1 33.3 %copy-start.4 = (bf16[64,2048]{1,0:T(8,128)(2,1)}, bf16[64,2048]{1,0:T(8,128)(2,1)S(1)}, u32[]{:S(2)}) copy-start(bf16[64,2048]{1,0:T(8,128)(2,1)S(1)} %collective-permute-done.3.refs_4_) | copy-start | bytes 786436
  15.1 33.2 %copy-start.5 = (bf16[64,2048]{1,0:T(8,128)(2,1)}, bf16[64,2048]{1,0:T(8,128)(2,1)S(1)}, u32[]{:S(2)}) copy-start(bf16[64,2048]{1,0:T(8,128)(2,1)S(1)} %collective-permute-done.1.refs_2_) | copy-start | bytes 786436
  15.1 8.2 %collective-permute-start.6 = (bf16[64,2048]{1,0:T(8,128)(2,1)S(1)}, bf16[64,2048]{1,0:T(8,128)(2,1)S(1)}, u32[]{:S(2)}, u32[]{:S(2)}) collective-permute-start(bf16[64,2048]{1,0:T(8,128)(2,1)S(1)} %collective-permute-done.1.refs_2_), channel_id=1, source_target_pairs={{0,8},{2,10},{8,16},{10,18},{16,24},{18,26},{24,28},{26,30},{28,20... | collective-permute-start | bytes 786440 | tf_op jit(solution)/shard_map/ppermute | solution.py:369
  15.4 7.9 %collective-permute-start.8 = (bf16[64,2048]{1,0:T(8,128)(2,1)S(1)}, bf16[64,2048]{1,0:T(8,128)(2,1)S(1)}, u32[]{:S(2)}, u32[]{:S(2)}) collective-permute-start(bf16[64,2048]{1,0:T(8,128)(2,1)S(1)} %collective-permute-done.3.refs_4_), channel_id=1, source_target_pairs={{0,4},{2,6},{8,0},{10,2},{16,8},{18,10},{24,16},{26,18},{28,24},{3... | collective-permute-start | bytes 786440 | tf_op jit(solution)/shard_map/ppermute | solution.py:370
  18.1 5.3 %collective-permute-start.10 = (bf16[128,256]{1,0:T(8,128)(2,1)S(1)}, bf16[128,256]{1,0:T(8,128)(2,1)S(1)}, u32[]{:S(2)}, u32[]{:S(2)}) collective-permute-start(bf16[128,256]{1,0:T(8,128)(2,1)S(1)} %get-tuple-element.42), channel_id=1, source_target_pairs={{0,8},{2,10},{4,12},{6,14},{8,0},{10,2},{12,4},{14,6},{16,24},{18,... | collective-permute-start | bytes 196616 | tf_op jit(solution)/shard_map/ppermute | solution.py:359
  23.3 25.0 %copy-start.6 = (bf16[64,2048]{1,0:T(8,128)(2,1)}, bf16[64,2048]{1,0:T(8,128)(2,1)S(1)}, u32[]{:S(2)}) copy-start(bf16[64,2048]{1,0:T(8,128)(2,1)S(1)} %collective-permute-done.6.refs_6_) | copy-start | bytes 786436
  23.4 25.0 %copy-start.7 = (bf16[64,2048]{1,0:T(8,128)(2,1)}, bf16[64,2048]{1,0:T(8,128)(2,1)S(1)}, u32[]{:S(2)}) copy-start(bf16[64,2048]{1,0:T(8,128)(2,1)S(1)} %collective-permute-done.8.refs_8_) | copy-start | bytes 786436
  23.4 8.3 %collective-permute-start.11 = (bf16[64,2048]{1,0:T(8,128)(2,1)S(1)}, bf16[64,2048]{1,0:T(8,128)(2,1)S(1)}, u32[]{:S(2)}, u32[]{:S(2)}) collective-permute-start(bf16[64,2048]{1,0:T(8,128)(2,1)S(1)} %collective-permute-done.6.refs_6_), channel_id=1, source_target_pairs={{0,8},{2,10},{8,16},{10,18},{16,24},{18,26},{24,28},{26,30},{28,20... | collective-permute-start | bytes 786440 | tf_op jit(solution)/shard_map/ppermute | solution.py:369
  23.7 8.5 %collective-permute-start.13 = (bf16[64,2048]{1,0:T(8,128)(2,1)S(1)}, bf16[64,2048]{1,0:T(8,128)(2,1)S(1)}, u32[]{:S(2)}, u32[]{:S(2)}) collective-permute-start(bf16[64,2048]{1,0:T(8,128)(2,1)S(1)} %collective-permute-done.8.refs_8_), channel_id=1, source_target_pairs={{0,4},{2,6},{8,0},{10,2},{16,8},{18,10},{24,16},{26,18},{28,24},{3... | collective-permute-start | bytes 786440 | tf_op jit(solution)/shard_map/ppermute | solution.py:370
  26.0 10.4 %collective-permute-start.19 = (bf16[256,128]{1,0:T(8,128)(2,1)S(1)}, bf16[256,128]{1,0:T(8,128)(2,1)S(1)}, u32[]{:S(2)}, u32[]{:S(2)}) collective-permute-start(bf16[256,128]{1,0:T(8,128)(2,1)S(1)} %get-tuple-element.41), channel_id=1, source_target_pairs={{0,4},{2,6},{4,0},{6,2},{8,12},{10,14},{12,8},{14,10},{16,20},{18,... | collective-permute-start | bytes 196616 | tf_op jit(solution)/shard_map/ppermute | solution.py:359
  31.7 16.7 %copy-start.2 = (bf16[64,2048]{1,0:T(8,128)(2,1)}, bf16[64,2048]{1,0:T(8,128)(2,1)S(1)}, u32[]{:S(2)}) copy-start(bf16[64,2048]{1,0:T(8,128)(2,1)S(1)} %collective-permute-done.11.refs_10_) | copy-start | bytes 786436
  31.7 5.2 %collective-permute-start.15 = (bf16[32,2048]{1,0:T(8,128)(2,1)S(1)}, bf16[32,2048]{1,0:T(8,128)(2,1)S(1)}, u32[]{:S(2)}, u32[]{:S(2)}) collective-permute-start(bf16[32,2048]{1,0:T(8,128)(2,1)S(1)} %slice.8), channel_id=1, source_target_pairs={{0,8},{2,10},{8,16},{10,18},{16,24},{18,26},{24,28},{26,30},{28,20... | collective-permute-start | bytes 393224 | tf_op jit(solution)/shard_map/ppermute | solution.py:376
  32.2 16.2 %copy-start.3 = (bf16[64,2048]{1,0:T(8,128)(2,1)}, bf16[64,2048]{1,0:T(8,128)(2,1)S(1)}, u32[]{:S(2)}) copy-start(bf16[64,2048]{1,0:T(8,128)(2,1)S(1)} %collective-permute-done.13.refs_12_) | copy-start | bytes 786436
  32.3 5.3 %collective-permute-start.17 = (bf16[32,2048]{1,0:T(8,128)(2,1)S(1)}, bf16[32,2048]{1,0:T(8,128)(2,1)S(1)}, u32[]{:S(2)}, u32[]{:S(2)}) collective-permute-start(bf16[32,2048]{1,0:T(8,128)(2,1)S(1)} %slice.9), channel_id=1, source_target_pairs={{0,4},{2,6},{8,0},{10,2},{16,8},{18,10},{24,16},{26,18},{28,24},{3... | collective-permute-start | bytes 393224 | tf_op jit(solution)/shard_map/ppermute | solution.py:377
  36.9 0.7 copy-start.15
  37.6 0.6 copy-start.16
  38.2 40.3 %all-to-all-start = ((bf16[16,64,512]{2,1,0:T(8,128)(2,1)}), bf16[16,64,512]{2,1,0:T(8,128)(2,1)S(1)}, u32[]{:S(2)}, u32[]{:S(2)}) async-start(bf16[16,64,512]{2,1,0:T(8,128)(2,1)} %split.1), calls=%async_computation | async-start | bytes 2097152 | tf_op jit(solution)/shard_map/all_to_all | solution.py:386
  43.5 1.6 %collective-permute-start = (bf16[64,2048]{1,0:T(8,128)(2,1)S(1)}, bf16[64,2048]{1,0:T(8,128)(2,1)S(1)}, u32[]{:S(2)}, u32[]{:S(2)}) collective-permute-start(bf16[64,2048]{1,0:T(8,128)(2,1)S(1)} %dynamic-slice_bitcast_fusion.refs_0_), channel_id=1, source_target_pairs={{0,2},{2,0},{8,10},{10,8},{16,18},{18,16},{24,26},{26,24},{28,30},... | collective-permute-start | bytes 786440 | tf_op jit(solution)/shard_map/ppermute | solution.py:349
  43.9 1.6 %collective-permute-start.4 = (bf16[64,2048]{1,0:T(8,128)(2,1)S(1)}, bf16[64,2048]{1,0:T(8,128)(2,1)S(1)}, u32[]{:S(2)}, u32[]{:S(2)}) collective-permute-start(bf16[64,2048]{1,0:T(8,128)(2,1)S(1)} %collective-permute-done.3.refs_4_), channel_id=1, source_target_pairs={{0,2},{2,0},{8,10},{10,8},{16,18},{18,16},{24,26},{26,24},{28,30},... | collective-permute-start | bytes 786440 | tf_op jit(solution)/shard_map/ppermute | solution.py:349
  44.1 1.8 %collective-permute-start.2 = (bf16[64,2048]{1,0:T(8,128)(2,1)S(1)}, bf16[64,2048]{1,0:T(8,128)(2,1)S(1)}, u32[]{:S(2)}, u32[]{:S(2)}) collective-permute-start(bf16[64,2048]{1,0:T(8,128)(2,1)S(1)} %collective-permute-done.1.refs_2_), channel_id=1, source_target_pairs={{0,2},{2,0},{8,10},{10,8},{16,18},{18,16},{24,26},{26,24},{28,30},... | collective-permute-start | bytes 786440 | tf_op jit(solution)/shard_map/ppermute | solution.py:349
  44.4 2.3 %collective-permute-start.7 = (bf16[64,2048]{1,0:T(8,128)(2,1)S(1)}, bf16[64,2048]{1,0:T(8,128)(2,1)S(1)}, u32[]{:S(2)}, u32[]{:S(2)}) collective-permute-start(bf16[64,2048]{1,0:T(8,128)(2,1)S(1)} %collective-permute-done.6.refs_6_), channel_id=1, source_target_pairs={{0,2},{2,0},{8,10},{10,8},{16,18},{18,16},{24,26},{26,24},{28,30},... | collective-permute-start | bytes 786440 | tf_op jit(solution)/shard_map/ppermute | solution.py:349
  44.6 1.8 %collective-permute-start.20 = (bf16[512,128]{1,0:T(8,128)(2,1)S(1)}, bf16[512,128]{1,0:T(8,128)(2,1)S(1)}, u32[]{:S(2)}, u32[]{:S(2)}) collective-permute-start(bf16[512,128]{1,0:T(8,128)(2,1)S(1)} %pad_maximum_fusion.1.refs_20_), channel_id=1, source_target_pairs={{0,2},{2,0},{8,10},{10,8},{16,18},{18,16},{24,26},{26,24},{28,30},... | collective-permute-start | bytes 393224 | tf_op jit(solution)/shard_map/ppermute | solution.py:383
  45.1 3.3 %copy-start.8 = (bf16[64,2048]{1,0:T(8,128)(2,1)}, bf16[64,2048]{1,0:T(8,128)(2,1)S(1)}, u32[]{:S(2)}) copy-start(bf16[64,2048]{1,0:T(8,128)(2,1)S(1)} %collective-permute-done.refs_1_) | copy-start | bytes 786436
  45.1 1.8 %collective-permute-start.9 = (bf16[64,2048]{1,0:T(8,128)(2,1)S(1)}, bf16[64,2048]{1,0:T(8,128)(2,1)S(1)}, u32[]{:S(2)}, u32[]{:S(2)}) collective-permute-start(bf16[64,2048]{1,0:T(8,128)(2,1)S(1)} %collective-permute-done.8.refs_8_), channel_id=1, source_target_pairs={{0,2},{2,0},{8,10},{10,8},{16,18},{18,16},{24,26},{26,24},{28,30},... | collective-permute-start | bytes 786440 | tf_op jit(solution)/shard_map/ppermute | solution.py:349
  45.5 3.0 %copy-start.9 = (bf16[64,2048]{1,0:T(8,128)(2,1)}, bf16[64,2048]{1,0:T(8,128)(2,1)S(1)}, u32[]{:S(2)}) copy-start(bf16[64,2048]{1,0:T(8,128)(2,1)S(1)} %collective-permute-done.4.refs_5_) | copy-start | bytes 786436
  45.5 2.9 %collective-permute-start.12 = (bf16[64,2048]{1,0:T(8,128)(2,1)S(1)}, bf16[64,2048]{1,0:T(8,128)(2,1)S(1)}, u32[]{:S(2)}, u32[]{:S(2)}) collective-permute-start(bf16[64,2048]{1,0:T(8,128)(2,1)S(1)} %collective-permute-done.11.refs_10_), channel_id=1, source_target_pairs={{0,2},{2,0},{8,10},{10,8},{16,18},{18,16},{24,26},{26,24},{28,30},... | collective-permute-start | bytes 786440 | tf_op jit(solution)/shard_map/ppermute | solution.py:349
  45.9 2.6 %copy-start.10 = (bf16[64,2048]{1,0:T(8,128)(2,1)}, bf16[64,2048]{1,0:T(8,128)(2,1)S(1)}, u32[]{:S(2)}) copy-start(bf16[64,2048]{1,0:T(8,128)(2,1)S(1)} %collective-permute-done.2.refs_3_) | copy-start | bytes 786436
  45.9 2.5 %collective-permute-start.14 = (bf16[64,2048]{1,0:T(8,128)(2,1)S(1)}, bf16[64,2048]{1,0:T(8,128)(2,1)S(1)}, u32[]{:S(2)}, u32[]{:S(2)}) collective-permute-start(bf16[64,2048]{1,0:T(8,128)(2,1)S(1)} %collective-permute-done.13.refs_12_), channel_id=1, source_target_pairs={{0,2},{2,0},{8,10},{10,8},{16,18},{18,16},{24,26},{26,24},{28,30},... | collective-permute-start | bytes 786440 | tf_op jit(solution)/shard_map/ppermute | solution.py:349
  46.4 1.6 %collective-permute-start.16 = (bf16[32,2048]{1,0:T(8,128)(2,1)}, bf16[32,2048]{1,0:T(8,128)(2,1)S(1)}, u32[]{:S(2)}, u32[]{:S(2)}) collective-permute-start(bf16[32,2048]{1,0:T(8,128)(2,1)} %copy-done.15), channel_id=1, source_target_pairs={{0,2},{2,0},{8,10},{10,8},{16,18},{18,16},{24,26},{26,24},{28,30},... | collective-permute-start | bytes 393224 | tf_op jit(solution)/shard_map/ppermute | solution.py:349
  46.8 1.7 %copy-start.11 = (bf16[64,2048]{1,0:T(8,128)(2,1)}, bf16[64,2048]{1,0:T(8,128)(2,1)S(1)}, u32[]{:S(2)}) copy-start(bf16[64,2048]{1,0:T(8,128)(2,1)S(1)} %collective-permute-done.7.refs_7_) | copy-start | bytes 786436
  46.8 1.6 %collective-permute-start.18 = (bf16[32,2048]{1,0:T(8,128)(2,1)}, bf16[32,2048]{1,0:T(8,128)(2,1)S(1)}, u32[]{:S(2)}, u32[]{:S(2)}) collective-permute-start(bf16[32,2048]{1,0:T(8,128)(2,1)} %copy-done.16), channel_id=1, source_target_pairs={{0,2},{2,0},{8,10},{10,8},{16,18},{18,16},{24,26},{26,24},{28,30},... | collective-permute-start | bytes 393224 | tf_op jit(solution)/shard_map/ppermute | solution.py:349
  46.9 1.5 %copy-start.12 = (bf16[64,2048]{1,0:T(8,128)(2,1)}, bf16[64,2048]{1,0:T(8,128)(2,1)S(1)}, u32[]{:S(2)}) copy-start(bf16[64,2048]{1,0:T(8,128)(2,1)S(1)} %collective-permute-done.9.refs_9_) | copy-start | bytes 786436
  48.0 0.7 copy-start.17
  48.3 0.7 copy-start.18
  48.4 0.7 copy-start.13
  49.1 0.7 copy-start.14
  76.9 27.9 %collective-permute-start.21 = (bf16[128,2048]{1,0:T(8,128)(2,1)S(1)}, bf16[128,2048]{1,0:T(8,128)(2,1)S(1)}, u32[]{:S(2)}, u32[]{:S(2)}) collective-permute-start(bf16[128,2048]{1,0:T(8,128)(2,1)S(1)} %get-tuple-element.33), channel_id=1, source_target_pairs={{0,1},{1,0},{2,3},{3,2},{4,5},{5,4},{6,7},{7,6},{8,9},{9,8},{10,11... | collective-permute-start | bytes 1572872 | tf_op jit(solution)/shard_map/ppermute | solution.py:391
  90.7 14.2 %collective-permute-start.22 = (bf16[64,2048]{1,0:T(8,128)(2,1)S(1)}, bf16[64,2048]{1,0:T(8,128)(2,1)S(1)}, u32[]{:S(2)}, u32[]{:S(2)}) collective-permute-start(bf16[64,2048]{1,0:T(8,128)(2,1)S(1)} %query_type.2), channel_id=1, source_target_pairs={{0,1},{1,0},{2,3},{3,2},{4,5},{5,4},{6,7},{7,6},{8,9},{9,8},{10,11... | collective-permute-start | bytes 786440 | tf_op jit(solution)/shard_map/ppermute | solution.py:391
  103.3 7.9 %collective-permute-start.23 = (bf16[64,2048]{1,0:T(8,128)(2,1)S(1)}, bf16[64,2048]{1,0:T(8,128)(2,1)S(1)}, u32[]{:S(2)}, u32[]{:S(2)}) collective-permute-start(bf16[64,2048]{1,0:T(8,128)(2,1)S(1)} %query_type.3), channel_id=1, source_target_pairs={{0,1},{1,0},{2,3},{3,2},{4,5},{5,4},{6,7},{7,6},{8,9},{9,8},{10,11... | collective-permute-start | bytes 786440 | tf_op jit(solution)/shard_map/ppermute | solution.py:391
where the time goes:
time: 113 us; the launch traced here: 112 us
  Pallas kernels  53.7 us (48%)
  starting transfers between devices  28.2 us (25%)
  waiting for transfers between devices  23 us (20%)
  local copies, waits for them, and re-layouts  4.2 us (4%)
  other arithmetic  2.27 us (2%)
    pallas_call x1, Pallas kernels, key_part(): pl.pallas_call(functools.partial(key_kernel, spots=tuple(spots), heads=he...  27.1 us
    pallas_call x2, Pallas kernels, query_part(): pl.pallas_call(functools.partial(query_kernel, heads=heads, chosen=chosen...  24.2 us
    ppermute x3, waiting for transfers between devices, halve(): got = lax.ppermute(leave, 'ctx', [(i, i ^ 2 * bit) for i in range(places)])  11.4 us
    ppermute x3, starting transfers between devices, by_sequence(): behind = lax.ppermute(behind, 'ctx', backward)  7.89 us
    ppermute x3, starting transfers between devices, halve(): got = lax.ppermute(leave, 'ctx', [(i, i ^ 2 * bit) for i in range(places)])  5.37 us
    all_to_all x1, starting transfers between devices, by_sequence(): lax.all_to_all(parts, 'ctx', 0, 0, tiled=True)  5.27 us
    ppermute x3, waiting for transfers between devices, swap(): return lax.ppermute(part, 'head', [(0, 1), (1, 0)])  5.15 us
    ppermute x3, starting transfers between devices, swap(): return lax.ppermute(part, 'head', [(0, 1), (1, 0)])  3.72 us
  transfers between devices with their start and end apart: 25, of which 11 were waited for; matrix products, arithmetic and copies ran while one was open for 2% of the time, Pallas kernels for 48%

commit v1 on v0

--- a/solution.py
+++ b/solution.py
@@ -18,10 +18,6 @@
 
 def dot(a, b, ca, cb):
     return lax.dot_general(a, b, (((ca,), (cb,)), ((), ())), preferred_element_type=jnp.float32)
-
-
-def turned(number, count):
-    return sum(((number >> bit) & 1) * (count >> (bit + 1)) for bit in range(count.bit_length() - 1))
 
 
 def rows_in(index, block):
@@ -199,7 +195,7 @@
         part = ref[...].astype(jnp.float32)
         part = jnp.where(core == 1, pltpu.roll(part, part.shape[1] // 2, 1), part).astype(jnp.bfloat16)
         for number in range(chips):
-            row = ((chip ^ turned(number, chips)) * 2 + (core + twin) % 2) * tokens
+            row = ((chip ^ (2 * (number % levels) + number // levels)) * 2 + (core + twin) % 2) * tokens
             here = pl.ds(pl.multiple_of(row, tokens), tokens)
             t_ref[here, :] = part[number * tokens : (number + 1) * tokens]
     for copy in copies:
@@ -265,10 +261,17 @@
     return [pltpu.with_memory_space_constraint(value, pltpu.HBM) for value in values]
 
 
+def in_vmem(*values):
+    return [pltpu.with_memory_space_constraint(value, pltpu.VMEM) for value in values]
+
+
 def key_part(pieces, spots, w_query, w_key, own, twin, heads):
     feats, width = w_key.shape
     rows = 2 * own.shape[0]
     score = pltpu.VMEM((rows, rows), jnp.float32)
+    late = [put(value) for put, value in zip((in_hbm, in_vmem) * 2 + (in_vmem,) * 4, pieces[-8:])]
+    late = [value for (value,) in late]
+    kept = [HBM] * (len(pieces) - 8) + [HBM, VMEM] * 2 + [VMEM] * 4
     return pl.pallas_call(
         functools.partial(
             key_kernel,
@@ -282,7 +285,7 @@
             pltpu.VMEM((rows, feats), jnp.bfloat16),
             jax.ShapeDtypeStruct((feats, width), jnp.bfloat16),
         ),
-        in_specs=[HBM] * (len(pieces) + 2) + [VMEM] * 2,
+        in_specs=kept + [HBM] * 2 + [VMEM] * 2,
         out_specs=(HBM, VMEM, VMEM),
         scratch_shapes=[
             pltpu.VMEM((rows, width), jnp.bfloat16),
@@ -299,7 +302,7 @@
         compiler_params=LIMIT,
         cost_estimate=cost(rows, heads),
         name="key_type",
-    )(*in_hbm(*pieces, w_query, w_key), own, twin)
+    )(*in_hbm(*pieces[:-8]), *late, *in_hbm(w_query, w_key), own, twin)
 
 
 def query_part(x, s, t, heads, chosen):
@@ -322,7 +325,7 @@
         compiler_params=LIMIT,
         cost_estimate=cost(rows, len(chosen)),
         name="query_type",
-    )(*in_hbm(x), pltpu.with_memory_space_constraint(s, pltpu.VMEM), t)
+    )(*in_hbm(x), *in_vmem(s), t)
 
 
 def by_sequence(teacher_q, teacher_k, student_in, w_query, w_key):
@@ -349,19 +352,23 @@
         pieces.extend((value, lax.ppermute(value, "ctx", twin)))
         spots.extend(((step, 0, offset), (step, 1, offset)))
 
-    chip = lax.axis_index("ctx") // 2
-
-    def halve(keys, bit):
-        width = keys.shape[1] // 2
-        mine = jnp.where(chip & bit, width, 0)
-        stay = lax.dynamic_slice_in_dim(keys, mine, width, 1)
-        leave = lax.dynamic_slice_in_dim(keys, width - mine, width, 1)
-        got = lax.ppermute(leave, "ctx", [(i, i ^ (2 * bit)) for i in range(places)])
-        return stay, got
+    where = lax.axis_index("ctx")
+    level, side = where // 4, where // 2 % 2
+    width = own_k.shape[1] // levels
+    keys = []
+    for other in range(levels):
+        piece = lax.dynamic_slice_in_dim(own_k, (level ^ other) * width, width, 1)
+        if other:
+            piece = lax.ppermute(piece, "ctx", [(i, i ^ (4 * other)) for i in range(places)])
+        keys.append(piece)
+
+    def across(keys):
+        low, high = keys[:, : width // 2], keys[:, width // 2 :]
+        stay, leave = jnp.where(side == 1, high, low), jnp.where(side == 1, low, high)
+        got = lax.ppermute(leave, "ctx", [(i, i ^ 2) for i in range(places)])
+        return jnp.concatenate([stay, got])
 
     half = tokens // 2
-    bits = [1 << bit for bit in reversed(range(count.bit_length() - 1))]
-    pair = halve(own_k, bits.pop(0))
     parts = split(teacher_q, places)
     keep(own_x, 0)
     ahead = behind = own_x
@@ -370,16 +377,13 @@
         behind = lax.ppermute(behind, "ctx", backward)
         keep(ahead, -step)
         keep(behind, step)
-        if bits:
-            ahead, behind, pair = lax.optimization_barrier((ahead, behind, pair))
-            pair = halve(jnp.concatenate(pair), bits.pop(0))
+        if step == count // 2 - 2:
+            ahead, behind, keys = lax.optimization_barrier((ahead, behind, keys))
+            keys = across(jnp.concatenate(keys))
     ahead = lax.ppermute(ahead[:half], "ctx", forward)
     behind = lax.ppermute(behind[half:], "ctx", backward)
     keep(ahead, -(count // 2))
     keep(behind, count // 2, half)
-    for bit in bits:
-        pair = halve(jnp.concatenate(pair), bit)
-    keys = jnp.concatenate(pair)
     twin_keys = lax.ppermute(keys, "ctx", twin)
 
     parts, _, keys = lax.optimization_barrier((parts, (ahead, behind), keys))
@@ -600,7 +604,7 @@
 
     def on_device(*args):
         batch, tokens, _ = args[0].shape
-        even = places in (4, 8, 16, 32) and tokens % 32 == 0
+        even = places in (8, 16, 32) and tokens % 32 == 0
         if even and batch == mesh.shape["head"] == 2 and tokens * places <= 1024:
             return by_sequence(*args)
         return by_rows(*args)

time: 113 us -> 110 us (0.973)
  local copies, waits for them, and re-layouts: 4.2 us -> 2.12 us
    ppermute x3 -> x4, waiting for transfers between devices: 11.4 us -> 4.18 us  [the longest x3 4.17 us: by_sequence(): lax.ppermute(piece, 'ctx', [(i, i ^ 4 * other) for i in range(places)])]
    ppermute x3, waiting for transfers between devices: 0.17 us -> 6.24 us  [by_sequence(): behind = lax.ppermute(behind, 'ctx', backward)]
    ppermute x3, starting transfers between devices: 7.89 us -> 4.74 us  [by_sequence(): behind = lax.ppermute(behind, 'ctx', backward)]
    ppermute x1, starting transfers between devices: 0.39 us -> 2.52 us  [by_sequence(): ahead = lax.ppermute(ahead[:half], 'ctx', forward)]
    unnamed x40 -> x29, local copies, waits for them, and re-layouts: 3.06 us -> 1.09 us
    ppermute x1, starting transfers between devices: 1.84 us -> 0.06 us  [by_sequence(): behind = lax.ppermute(behind[half:], 'ctx', backward)]
    ppermute x3, starting transfers between devices: 0.78 us -> 2.54 us  [by_sequence(): ahead = lax.ppermute(ahead, 'ctx', forward)]
    ppermute x1, waiting for transfers between devices: 0.64 us -> 2.31 us  [by_sequence(): behind = lax.ppermute(behind[half:], 'ctx', backward)]
  transfers between devices with their start and end apart: 25 -> 26, of which waited for: 11 -> 12; matrix products, arithmetic and copies ran while one was open for 2% -> 2% of each run, Pallas kernels for 48% -> 49%
where the time goes in v1:
time: 110 us; the launch traced here: 109 us
  Pallas kernels  53.6 us (49%)
  starting transfers between devices  27.1 us (25%)
  waiting for transfers between devices  23.2 us (21%)
  other arithmetic  2.28 us (2%)
  local copies, waits for them, and re-layouts  2.12 us (2%)
    pallas_call x1, Pallas kernels, key_part(): pl.pallas_call(functools.partial(key_kernel, spots=tuple(spots), heads=he...  27 us
    pallas_call x2, Pallas kernels, query_part(): pl.pallas_call(functools.partial(query_kernel, heads=heads, chosen=chosen...  24.2 us
    ppermute x3, waiting for transfers between devices, by_sequence(): behind = lax.ppermute(behind, 'ctx', backward)  6.24 us
    ppermute x3, waiting for transfers between devices, swap(): return lax.ppermute(part, 'head', [(0, 1), (1, 0)])  5.31 us
    ppermute x3, starting transfers between devices, by_sequence(): behind = lax.ppermute(behind, 'ctx', backward)  4.74 us
    ppermute x3, starting transfers between devices, by_sequence(): lax.ppermute(piece, 'ctx', [(i, i ^ 4 * other) for i in range(places)])  4.47 us
    ppermute x3, waiting for transfers between devices, by_sequence(): lax.ppermute(piece, 'ctx', [(i, i ^ 4 * other) for i in range(places)])  4.17 us
    all_to_all x1, starting transfers between devices, by_sequence(): lax.all_to_all(parts, 'ctx', 0, 0, tiled=True)  4.04 us
  transfers between devices with their start and end apart: 26, of which 12 were waited for; matrix products, arithmetic and copies ran while one was open for 2% of the time, Pallas kernels for 49%

profile of v1, /device:TPU:0, one launch (start us, length us, event | category | flops | bytes accessed | tf_op | source)
XLA Modules:
  0.0 109.2 jit_solution(6604683623253725752)
XLA Ops:
  0.6 1.0 copy-done
  1.7 3.0 %collective-permute-start.3 = (bf16[64,2048]{1,0:T(8,128)(2,1)S(1)}, bf16[64,2048]{1,0:T(8,128)(2,1)S(1)}, u32[]{:S(2)}, u32[]{:S(2)}) collective-permute-start(bf16[64,2048]{1,0:T(8,128)(2,1)S(1)} %dynamic-slice_bitcast_fusion.refs_0_), channel_id=1, source_target_pairs={{0,4},{2,6},{8,0},{10,2},{16,8},{18,10},{24,16},{26,18},{28,24},{3... | collective-permute-start | bytes 786440 | tf_op jit(solution)/shard_map/ppermute | solution.py:377
  4.7 0.1 collective-permute-start.1
  4.9 6.2 %collective-permute-done.3.refs_4_ = bf16[64,2048]{1,0:T(8,128)(2,1)S(1)} collective-permute-done((bf16[64,2048]{1,0:T(8,128)(2,1)S(1)}, bf16[64,2048]{1,0:T(8,128)(2,1)S(1)}, u32[]{:S(2)}, u32[]{:S(2)}) %collective-permute-start.3) | collective-permute-done | bytes 262176 | tf_op jit(solution)/shard_map/ppermute | solution.py:377
  11.1 1.7 %collective-permute-start.7 = (bf16[64,2048]{1,0:T(8,128)(2,1)S(1)}, bf16[64,2048]{1,0:T(8,128)(2,1)S(1)}, u32[]{:S(2)}, u32[]{:S(2)}) collective-permute-start(bf16[64,2048]{1,0:T(8,128)(2,1)S(1)} %collective-permute-done.3.refs_4_), channel_id=1, source_target_pairs={{0,4},{2,6},{8,0},{10,2},{16,8},{18,10},{24,16},{26,18},{28,24},{3... | collective-permute-start | bytes 786440 | tf_op jit(solution)/shard_map/ppermute | solution.py:377
  12.8 0.3 collective-permute-start.5
  13.1 1.0 dynamic-slice_bitcast_fusion.1
  14.1 3.8 %collective-permute-start.11 = (bf16[64,256]{1,0:T(8,128)(2,1)S(1)}, bf16[64,256]{1,0:T(8,128)(2,1)S(1)}, u32[]{:S(2)}, u32[]{:S(2)}) collective-permute-start(bf16[64,256]{1,0:T(8,128)(2,1)S(1)} %get-tuple-element.34), channel_id=1, source_target_pairs={{0,24},{2,26},{4,28},{6,30},{8,16},{10,18},{12,20},{14,22},{16,8},... | collective-permute-start | bytes 98312 | tf_op jit(solution)/shard_map/ppermute | solution.py:362
  17.9 0.6 collective-permute-start.10
  18.6 3.4 %collective-permute-done.11 = bf16[64,256]{1,0:T(8,128)(2,1)S(1)} collective-permute-done((bf16[64,256]{1,0:T(8,128)(2,1)S(1)}, bf16[64,256]{1,0:T(8,128)(2,1)S(1)}, u32[]{:S(2)}, u32[]{:S(2)}) %collective-permute-start.11) | collective-permute-done | bytes 32800 | tf_op jit(solution)/shard_map/ppermute | solution.py:362
  22.0 0.2 collective-permute-done.9
  22.2 0.6 collective-permute-done.10
  22.8 2.1 %collective-permute-start.12 = (bf16[64,2048]{1,0:T(8,128)(2,1)S(1)}, bf16[64,2048]{1,0:T(8,128)(2,1)S(1)}, u32[]{:S(2)}, u32[]{:S(2)}) collective-permute-start(bf16[64,2048]{1,0:T(8,128)(2,1)S(1)} %collective-permute-done.5.refs_6_), channel_id=1, source_target_pairs={{0,8},{2,10},{8,16},{10,18},{16,24},{18,26},{24,28},{26,30},{28,20... | collective-permute-start | bytes 786440 | tf_op jit(solution)/shard_map/ppermute | solution.py:376
  24.9 0.0 collective-permute-start.14
  24.9 2.0 %collective-permute-start.20 = (bf16[256,128]{1,0:T(8,128)(2,1)S(1)}, bf16[256,128]{1,0:T(8,128)(2,1)S(1)}, u32[]{:S(2)}, u32[]{:S(2)}) collective-permute-start(bf16[256,128]{1,0:T(8,128)(2,1)S(1)} %get-tuple-element.39), channel_id=1, source_target_pairs={{0,4},{2,6},{4,0},{6,2},{8,12},{10,14},{12,8},{14,10},{16,20},{18,... | collective-permute-start | bytes 196616 | tf_op jit(solution)/shard_map/ppermute | solution.py:368
  27.0 3.1 %collective-permute-done.12.refs_10_ = bf16[64,2048]{1,0:T(8,128)(2,1)S(1)} collective-permute-done((bf16[64,2048]{1,0:T(8,128)(2,1)S(1)}, bf16[64,2048]{1,0:T(8,128)(2,1)S(1)}, u32[]{:S(2)}, u32[]{:S(2)}) %collective-permute-start.12) | collective-permute-done | bytes 262176 | tf_op jit(solution)/shard_map/ppermute | solution.py:376
  30.1 2.5 %collective-permute-start.16 = (bf16[32,2048]{1,0:T(8,128)(2,1)S(1)}, bf16[32,2048]{1,0:T(8,128)(2,1)S(1)}, u32[]{:S(2)}, u32[]{:S(2)}) collective-permute-start(bf16[32,2048]{1,0:T(8,128)(2,1)S(1)} %slice.16), channel_id=1, source_target_pairs={{0,8},{2,10},{8,16},{10,18},{16,24},{18,26},{24,28},{26,30},{28,20... | collective-permute-start | bytes 393224 | tf_op jit(solution)/shard_map/ppermute | solution.py:383
  32.6 0.1 collective-permute-start.18
  32.7 2.4 %split.1 = bf16[16,64,512]{2,1,0:T(8,128)(2,1)} custom-call(bf16[2,64,8192]{2,1,0:T(8,128)(2,1)} %t_ref.1), custom_call_target="tpu_custom_call" | custom-call | tf_op jit(solution)/shard_map/split/pallas_call | solution.py:159
  35.1 0.2 collective-permute-done.16.refs_14_
  35.4 2.3 %collective-permute-done.18.refs_16_ = bf16[32,2048]{1,0:T(8,128)(2,1)S(1)} collective-permute-done((bf16[32,2048]{1,0:T(8,128)(2,1)S(1)}, bf16[32,2048]{1,0:T(8,128)(2,1)S(1)}, u32[]{:S(2)}, u32[]{:S(2)}) %collective-permute-start.18) | collective-permute-done | bytes 131104 | tf_op jit(solution)/shard_map/ppermute | solution.py:384
  37.7 4.0 %all-to-all-start = ((bf16[16,64,512]{2,1,0:T(8,128)(2,1)}), bf16[16,64,512]{2,1,0:T(8,128)(2,1)S(1)}, u32[]{:S(2)}, u32[]{:S(2)}) async-start(bf16[16,64,512]{2,1,0:T(8,128)(2,1)} %split.1), calls=%async_computation | async-start | bytes 2097152 | tf_op jit(solution)/shard_map/all_to_all | solution.py:390
  41.7 0.4 collective-permute-start
  42.1 0.2 collective-permute-start.4
  42.3 0.3 collective-permute-start.2
  42.6 0.2 collective-permute-start.8
  42.8 0.3 collective-permute-start.21
  43.1 0.2 collective-permute-done.refs_1_
  43.3 0.3 collective-permute-start.6
  43.7 0.0 collective-permute-done.4.refs_5_
  43.7 0.3 collective-permute-start.13
  44.0 0.6 collective-permute-done.2.refs_3_
  44.6 0.4 collective-permute-start.15
  45.0 0.1 collective-permute-start.17
  45.1 0.4 collective-permute-start.19
  45.5 0.8 collective-permute-done.17.refs_15_
  46.4 0.2 collective-permute-done.19.refs_17_
  46.6 27.0 %key_type.1 = (bf16[1024,2048]{1,0:T(8,128)(2,1)}, bf16[1024,128]{1,0:T(8,128)(2,1)S(1)}, bf16[128,2048]{1,0:T(8,128)(2,1)S(1)}) custom-call(bf16[64,2048]{1,0:T(8,128)(2,1)} %copy-done.1, bf16[64,2048]{1,0:T(8,128)(2,1)} %copy-done.8, bf16[64,2048]{1,0:T(8,128)(2,1)} %copy-done.5, bf16[64,2048]{1,0:T(8,128)(2,1)} %copy-done.10, bf16[64,2048]{1,0:T(8,128)(2,1)} %copy-done.4, ...), custom_call_target="tpu_custom_call" | custom-call | flops 6442450944 | bytes 4194304 | tf_op jit(solution)/shard_map/key_type/pallas_call | solution.py:275
  73.7 1.6 %collective-permute-start.22 = (bf16[128,2048]{1,0:T(8,128)(2,1)S(1)}, bf16[128,2048]{1,0:T(8,128)(2,1)S(1)}, u32[]{:S(2)}, u32[]{:S(2)}) collective-permute-start(bf16[128,2048]{1,0:T(8,128)(2,1)S(1)} %get-tuple-element.29), channel_id=1, source_target_pairs={{0,1},{1,0},{2,3},{3,2},{4,5},{5,4},{6,7},{7,6},{8,9},{9,8},{10,11... | collective-permute-start | bytes 1572872 | tf_op jit(solution)/shard_map/ppermute | solution.py:395
  75.3 12.2 %query_type.2 = bf16[64,2048]{1,0:T(8,128)(2,1)S(1)} custom-call(bf16[1024,2048]{1,0:T(8,128)(2,1)} %get-tuple-element.26.x_hbm, bf16[1024,128]{1,0:T(8,128)(2,1)S(1)} %get-tuple-element.30.s_ref, bf16[1024,512]{1,0:T(8,128)(2,1)S(1)} %bitcast.11), custom_call_target="tpu_custom_call" | custom-call | flops 3221225472 | bytes 4194304 | tf_op jit(solution)/shard_map/query_type/pallas_call | solution.py:312
  87.5 0.6 collective-permute-start.23
  88.1 12.0 %query_type.3 = bf16[64,2048]{1,0:T(8,128)(2,1)S(1)} custom-call(bf16[1024,2048]{1,0:T(8,128)(2,1)} %get-tuple-element.26.x_hbm, bf16[1024,128]{1,0:T(8,128)(2,1)S(1)} %get-tuple-element.30.s_ref, bf16[1024,512]{1,0:T(8,128)(2,1)S(1)} %bitcast.12), custom_call_target="tpu_custom_call" | custom-call | flops 3221225472 | bytes 4194304 | tf_op jit(solution)/shard_map/query_type/pallas_call | solution.py:312
  100.1 1.6 %collective-permute-start.24 = (bf16[64,2048]{1,0:T(8,128)(2,1)S(1)}, bf16[64,2048]{1,0:T(8,128)(2,1)S(1)}, u32[]{:S(2)}, u32[]{:S(2)}) collective-permute-start(bf16[64,2048]{1,0:T(8,128)(2,1)S(1)} %query_type.3), channel_id=1, source_target_pairs={{0,1},{1,0},{2,3},{3,2},{4,5},{5,4},{6,7},{7,6},{8,9},{9,8},{10,11... | collective-permute-start | bytes 786440 | tf_op jit(solution)/shard_map/ppermute | solution.py:395
  101.7 1.1 %convert_add_fusion = f32[128,2048]{1,0:T(8,128)} fusion(bf16[128,2048]{1,0:T(8,128)(2,1)S(1)} %collective-permute-done.22, bf16[128,2048]{1,0:T(8,128)(2,1)S(1)} %get-tuple-element.29), kind=kLoop, calls=%fused_computation.1 | loop fusion | flops 786432 | bytes 2097152 | tf_op jit(solution)/shard_map/add | solution.py:398
  102.8 0.1 convert_add_fusion.2
  102.8 5.3 %collective-permute-done.24 = bf16[64,2048]{1,0:T(8,128)(2,1)S(1)} collective-permute-done((bf16[64,2048]{1,0:T(8,128)(2,1)S(1)}, bf16[64,2048]{1,0:T(8,128)(2,1)S(1)}, u32[]{:S(2)}, u32[]{:S(2)}) %collective-permute-start.24) | collective-permute-done | bytes 262176 | tf_op jit(solution)/shard_map/ppermute | solution.py:395
  108.1 0.1 convert_add_fusion.1
  108.2 1.0 pad_maximum_fusion
  (48 shorter events, 0.2 us)
Async XLA Ops:
  0.6 1.0 copy-start
  1.7 44.9 %copy-start.1 = (bf16[64,2048]{1,0:T(8,128)(2,1)}, bf16[64,2048]{1,0:T(8,128)(2,1)S(1)}, u32[]{:S(2)}) copy-start(bf16[64,2048]{1,0:T(8,128)(2,1)S(1)} %dynamic-slice_bitcast_fusion.refs_0_) | copy-start | bytes 786436
  1.7 9.4 %collective-permute-start.3 = (bf16[64,2048]{1,0:T(8,128)(2,1)S(1)}, bf16[64,2048]{1,0:T(8,128)(2,1)S(1)}, u32[]{:S(2)}, u32[]{:S(2)}) collective-permute-start(bf16[64,2048]{1,0:T(8,128)(2,1)S(1)} %dynamic-slice_bitcast_fusion.refs_0_), channel_id=1, source_target_pairs={{0,4},{2,6},{8,0},{10,2},{16,8},{18,10},{24,16},{26,18},{28,24},{3... | collective-permute-start | bytes 786440 | tf_op jit(solution)/shard_map/ppermute | solution.py:377
  4.7 8.1 %collective-permute-start.1 = (bf16[64,2048]{1,0:T(8,128)(2,1)S(1)}, bf16[64,2048]{1,0:T(8,128)(2,1)S(1)}, u32[]{:S(2)}, u32[]{:S(2)}) collective-permute-start(bf16[64,2048]{1,0:T(8,128)(2,1)S(1)} %dynamic-slice_bitcast_fusion.refs_0_), channel_id=1, source_target_pairs={{0,8},{2,10},{8,16},{10,18},{16,24},{18,26},{24,28},{26,30},{28,20... | collective-permute-start | bytes 786440 | tf_op jit(solution)/shard_map/ppermute | solution.py:376
  11.1 35.5 %copy-start.4 = (bf16[64,2048]{1,0:T(8,128)(2,1)}, bf16[64,2048]{1,0:T(8,128)(2,1)S(1)}, u32[]{:S(2)}) copy-start(bf16[64,2048]{1,0:T(8,128)(2,1)S(1)} %collective-permute-done.3.refs_4_) | copy-start | bytes 786436
  11.1 11.7 %collective-permute-start.7 = (bf16[64,2048]{1,0:T(8,128)(2,1)S(1)}, bf16[64,2048]{1,0:T(8,128)(2,1)S(1)}, u32[]{:S(2)}, u32[]{:S(2)}) collective-permute-start(bf16[64,2048]{1,0:T(8,128)(2,1)S(1)} %collective-permute-done.3.refs_4_), channel_id=1, source_target_pairs={{0,4},{2,6},{8,0},{10,2},{16,8},{18,10},{24,16},{26,18},{28,24},{3... | collective-permute-start | bytes 786440 | tf_op jit(solution)/shard_map/ppermute | solution.py:377
  12.8 17.3 %copy-start.5 = (bf16[64,2048]{1,0:T(8,128)(2,1)}, bf16[64,2048]{1,0:T(8,128)(2,1)S(1)}, u32[]{:S(2)}) copy-start(bf16[64,2048]{1,0:T(8,128)(2,1)S(1)} %collective-permute-done.1.refs_2_) | copy-start | bytes 786436
  12.8 10.0 %collective-permute-start.5 = (bf16[64,2048]{1,0:T(8,128)(2,1)S(1)}, bf16[64,2048]{1,0:T(8,128)(2,1)S(1)}, u32[]{:S(2)}, u32[]{:S(2)}) collective-permute-start(bf16[64,2048]{1,0:T(8,128)(2,1)S(1)} %collective-permute-done.1.refs_2_), channel_id=1, source_target_pairs={{0,8},{2,10},{8,16},{10,18},{16,24},{18,26},{24,28},{26,30},{28,20... | collective-permute-start | bytes 786440 | tf_op jit(solution)/shard_map/ppermute | solution.py:376
  14.1 7.9 %collective-permute-start.11 = (bf16[64,256]{1,0:T(8,128)(2,1)S(1)}, bf16[64,256]{1,0:T(8,128)(2,1)S(1)}, u32[]{:S(2)}, u32[]{:S(2)}) collective-permute-start(bf16[64,256]{1,0:T(8,128)(2,1)S(1)} %get-tuple-element.34), channel_id=1, source_target_pairs={{0,24},{2,26},{4,28},{6,30},{8,16},{10,18},{12,20},{14,22},{16,8},... | collective-permute-start | bytes 98312 | tf_op jit(solution)/shard_map/ppermute | solution.py:362
  17.9 4.3 %collective-permute-start.9 = (bf16[64,256]{1,0:T(8,128)(2,1)S(1)}, bf16[64,256]{1,0:T(8,128)(2,1)S(1)}, u32[]{:S(2)}, u32[]{:S(2)}) collective-permute-start(bf16[64,256]{1,0:T(8,128)(2,1)S(1)} %get-tuple-element.35), channel_id=1, source_target_pairs={{0,8},{2,10},{4,12},{6,14},{8,0},{10,2},{12,4},{14,6},{16,24},{18,... | collective-permute-start | bytes 98312 | tf_op jit(solution)/shard_map/ppermute | solution.py:362
  17.9 4.8 %collective-permute-start.10 = (bf16[64,256]{1,0:T(8,128)(2,1)S(1)}, bf16[64,256]{1,0:T(8,128)(2,1)S(1)}, u32[]{:S(2)}, u32[]{:S(2)}) collective-permute-start(bf16[64,256]{1,0:T(8,128)(2,1)S(1)} %get-tuple-element.37), channel_id=1, source_target_pairs={{0,16},{2,18},{4,20},{6,22},{8,24},{10,26},{12,28},{14,30},{16,0},... | collective-permute-start | bytes 98312 | tf_op jit(solution)/shard_map/ppermute | solution.py:362
  22.8 23.8 %copy-start.6 = (bf16[64,2048]{1,0:T(8,128)(2,1)}, bf16[64,2048]{1,0:T(8,128)(2,1)S(1)}, u32[]{:S(2)}) copy-start(bf16[64,2048]{1,0:T(8,128)(2,1)S(1)} %collective-permute-done.7.refs_8_) | copy-start | bytes 786436
  22.8 23.8 %copy-start.7 = (bf16[64,2048]{1,0:T(8,128)(2,1)}, bf16[64,2048]{1,0:T(8,128)(2,1)S(1)}, u32[]{:S(2)}) copy-start(bf16[64,2048]{1,0:T(8,128)(2,1)S(1)} %collective-permute-done.5.refs_6_) | copy-start | bytes 786436
  22.8 7.3 %collective-permute-start.12 = (bf16[64,2048]{1,0:T(8,128)(2,1)S(1)}, bf16[64,2048]{1,0:T(8,128)(2,1)S(1)}, u32[]{:S(2)}, u32[]{:S(2)}) collective-permute-start(bf16[64,2048]{1,0:T(8,128)(2,1)S(1)} %collective-permute-done.5.refs_6_), channel_id=1, source_target_pairs={{0,8},{2,10},{8,16},{10,18},{16,24},{18,26},{24,28},{26,30},{28,20... | collective-permute-start | bytes 786440 | tf_op jit(solution)/shard_map/ppermute | solution.py:376
  24.9 7.8 %collective-permute-start.14 = (bf16[64,2048]{1,0:T(8,128)(2,1)S(1)}, bf16[64,2048]{1,0:T(8,128)(2,1)S(1)}, u32[]{:S(2)}, u32[]{:S(2)}) collective-permute-start(bf16[64,2048]{1,0:T(8,128)(2,1)S(1)} %collective-permute-done.7.refs_8_), channel_id=1, source_target_pairs={{0,4},{2,6},{8,0},{10,2},{16,8},{18,10},{24,16},{26,18},{28,24},{3... | collective-permute-start | bytes 786440 | tf_op jit(solution)/shard_map/ppermute | solution.py:377
  24.9 10.2 %collective-permute-start.20 = (bf16[256,128]{1,0:T(8,128)(2,1)S(1)}, bf16[256,128]{1,0:T(8,128)(2,1)S(1)}, u32[]{:S(2)}, u32[]{:S(2)}) collective-permute-start(bf16[256,128]{1,0:T(8,128)(2,1)S(1)} %get-tuple-element.39), channel_id=1, source_target_pairs={{0,4},{2,6},{4,0},{6,2},{8,12},{10,14},{12,8},{14,10},{16,20},{18,... | collective-permute-start | bytes 196616 | tf_op jit(solution)/shard_map/ppermute | solution.py:368
  30.1 16.5 %copy-start.2 = (bf16[64,2048]{1,0:T(8,128)(2,1)}, bf16[64,2048]{1,0:T(8,128)(2,1)S(1)}, u32[]{:S(2)}) copy-start(bf16[64,2048]{1,0:T(8,128)(2,1)S(1)} %collective-permute-done.12.refs_10_) | copy-start | bytes 786436
  30.1 5.2 %collective-permute-start.16 = (bf16[32,2048]{1,0:T(8,128)(2,1)S(1)}, bf16[32,2048]{1,0:T(8,128)(2,1)S(1)}, u32[]{:S(2)}, u32[]{:S(2)}) collective-permute-start(bf16[32,2048]{1,0:T(8,128)(2,1)S(1)} %slice.16), channel_id=1, source_target_pairs={{0,8},{2,10},{8,16},{10,18},{16,24},{18,26},{24,28},{26,30},{28,20... | collective-permute-start | bytes 393224 | tf_op jit(solution)/shard_map/ppermute | solution.py:383
  32.6 14.0 %copy-start.3 = (bf16[64,2048]{1,0:T(8,128)(2,1)}, bf16[64,2048]{1,0:T(8,128)(2,1)S(1)}, u32[]{:S(2)}) copy-start(bf16[64,2048]{1,0:T(8,128)(2,1)S(1)} %collective-permute-done.14.refs_12_) | copy-start | bytes 786436
  32.6 5.0 %collective-permute-start.18 = (bf16[32,2048]{1,0:T(8,128)(2,1)S(1)}, bf16[32,2048]{1,0:T(8,128)(2,1)S(1)}, u32[]{:S(2)}, u32[]{:S(2)}) collective-permute-start(bf16[32,2048]{1,0:T(8,128)(2,1)S(1)} %slice.17), channel_id=1, source_target_pairs={{0,4},{2,6},{8,0},{10,2},{16,8},{18,10},{24,16},{26,18},{28,24},{3... | collective-permute-start | bytes 393224 | tf_op jit(solution)/shard_map/ppermute | solution.py:384
  37.7 37.6 %all-to-all-start = ((bf16[16,64,512]{2,1,0:T(8,128)(2,1)}), bf16[16,64,512]{2,1,0:T(8,128)(2,1)S(1)}, u32[]{:S(2)}, u32[]{:S(2)}) async-start(bf16[16,64,512]{2,1,0:T(8,128)(2,1)} %split.1), calls=%async_computation | async-start | bytes 2097152 | tf_op jit(solution)/shard_map/all_to_all | solution.py:390
  41.7 1.6 %collective-permute-start = (bf16[64,2048]{1,0:T(8,128)(2,1)S(1)}, bf16[64,2048]{1,0:T(8,128)(2,1)S(1)}, u32[]{:S(2)}, u32[]{:S(2)}) collective-permute-start(bf16[64,2048]{1,0:T(8,128)(2,1)S(1)} %dynamic-slice_bitcast_fusion.refs_0_), channel_id=1, source_target_pairs={{0,2},{2,0},{8,10},{10,8},{16,18},{18,16},{24,26},{26,24},{28,30},... | collective-permute-start | bytes 786440 | tf_op jit(solution)/shard_map/ppermute | solution.py:352
  42.1 1.6 %collective-permute-start.4 = (bf16[64,2048]{1,0:T(8,128)(2,1)S(1)}, bf16[64,2048]{1,0:T(8,128)(2,1)S(1)}, u32[]{:S(2)}, u32[]{:S(2)}) collective-permute-start(bf16[64,2048]{1,0:T(8,128)(2,1)S(1)} %collective-permute-done.3.refs_4_), channel_id=1, source_target_pairs={{0,2},{2,0},{8,10},{10,8},{16,18},{18,16},{24,26},{26,24},{28,30},... | collective-permute-start | bytes 786440 | tf_op jit(solution)/shard_map/ppermute | solution.py:352
  42.3 2.3 %collective-permute-start.2 = (bf16[64,2048]{1,0:T(8,128)(2,1)}, bf16[64,2048]{1,0:T(8,128)(2,1)S(1)}, u32[]{:S(2)}, u32[]{:S(2)}) collective-permute-start(bf16[64,2048]{1,0:T(8,128)(2,1)} %copy-done.5), channel_id=1, source_target_pairs={{0,2},{2,0},{8,10},{10,8},{16,18},{18,16},{24,26},{26,24},{28,30},... | collective-permute-start | bytes 786440 | tf_op jit(solution)/shard_map/ppermute | solution.py:352
  42.6 2.5 %collective-permute-start.8 = (bf16[64,2048]{1,0:T(8,128)(2,1)S(1)}, bf16[64,2048]{1,0:T(8,128)(2,1)S(1)}, u32[]{:S(2)}, u32[]{:S(2)}) collective-permute-start(bf16[64,2048]{1,0:T(8,128)(2,1)S(1)} %collective-permute-done.7.refs_8_), channel_id=1, source_target_pairs={{0,2},{2,0},{8,10},{10,8},{16,18},{18,16},{24,26},{26,24},{28,30},... | collective-permute-start | bytes 786440 | tf_op jit(solution)/shard_map/ppermute | solution.py:352
  42.8 2.2 %collective-permute-start.21 = (bf16[512,128]{1,0:T(8,128)(2,1)S(1)}, bf16[512,128]{1,0:T(8,128)(2,1)S(1)}, u32[]{:S(2)}, u32[]{:S(2)}) collective-permute-start(bf16[512,128]{1,0:T(8,128)(2,1)S(1)} %pad_maximum_fusion.1.refs_20_), channel_id=1, source_target_pairs={{0,2},{2,0},{8,10},{10,8},{16,18},{18,16},{24,26},{26,24},{28,30},... | collective-permute-start | bytes 393224 | tf_op jit(solution)/shard_map/ppermute | solution.py:387
  43.3 3.3 %copy-start.8 = (bf16[64,2048]{1,0:T(8,128)(2,1)}, bf16[64,2048]{1,0:T(8,128)(2,1)S(1)}, u32[]{:S(2)}) copy-start(bf16[64,2048]{1,0:T(8,128)(2,1)S(1)} %collective-permute-done.refs_1_) | copy-start | bytes 786436
  43.3 2.2 %collective-permute-start.6 = (bf16[64,2048]{1,0:T(8,128)(2,1)S(1)}, bf16[64,2048]{1,0:T(8,128)(2,1)S(1)}, u32[]{:S(2)}, u32[]{:S(2)}) collective-permute-start(bf16[64,2048]{1,0:T(8,128)(2,1)S(1)} %collective-permute-done.5.refs_6_), channel_id=1, source_target_pairs={{0,2},{2,0},{8,10},{10,8},{16,18},{18,16},{24,26},{26,24},{28,30},... | collective-permute-start | bytes 786440 | tf_op jit(solution)/shard_map/ppermute | solution.py:352
  43.7 2.9 %copy-start.9 = (bf16[64,2048]{1,0:T(8,128)(2,1)}, bf16[64,2048]{1,0:T(8,128)(2,1)S(1)}, u32[]{:S(2)}) copy-start(bf16[64,2048]{1,0:T(8,128)(2,1)S(1)} %collective-permute-done.4.refs_5_) | copy-start | bytes 786436
  43.7 2.8 %collective-permute-start.13 = (bf16[64,2048]{1,0:T(8,128)(2,1)S(1)}, bf16[64,2048]{1,0:T(8,128)(2,1)S(1)}, u32[]{:S(2)}, u32[]{:S(2)}) collective-permute-start(bf16[64,2048]{1,0:T(8,128)(2,1)S(1)} %collective-permute-done.12.refs_10_), channel_id=1, source_target_pairs={{0,2},{2,0},{8,10},{10,8},{16,18},{18,16},{24,26},{26,24},{28,30},... | collective-permute-start | bytes 786440 | tf_op jit(solution)/shard_map/ppermute | solution.py:352
  44.6 2.0 %copy-start.10 = (bf16[64,2048]{1,0:T(8,128)(2,1)}, bf16[64,2048]{1,0:T(8,128)(2,1)S(1)}, u32[]{:S(2)}) copy-start(bf16[64,2048]{1,0:T(8,128)(2,1)S(1)} %collective-permute-done.2.refs_3_) | copy-start | bytes 786436
  44.6 1.9 %collective-permute-start.15 = (bf16[64,2048]{1,0:T(8,128)(2,1)S(1)}, bf16[64,2048]{1,0:T(8,128)(2,1)S(1)}, u32[]{:S(2)}, u32[]{:S(2)}) collective-permute-start(bf16[64,2048]{1,0:T(8,128)(2,1)S(1)} %collective-permute-done.14.refs_12_), channel_id=1, source_target_pairs={{0,2},{2,0},{8,10},{10,8},{16,18},{18,16},{24,26},{26,24},{28,30},... | collective-permute-start | bytes 786440 | tf_op jit(solution)/shard_map/ppermute | solution.py:352
  45.0 1.3 %collective-permute-start.17 = (bf16[32,2048]{1,0:T(8,128)(2,1)S(1)}, bf16[32,2048]{1,0:T(8,128)(2,1)S(1)}, u32[]{:S(2)}, u32[]{:S(2)}) collective-permute-start(bf16[32,2048]{1,0:T(8,128)(2,1)S(1)} %collective-permute-done.16.refs_14_), channel_id=1, source_target_pairs={{0,2},{2,0},{8,10},{10,8},{16,18},{18,16},{24,26},{26,24},{28,30},... | collective-permute-start | bytes 393224 | tf_op jit(solution)/shard_map/ppermute | solution.py:352
  45.1 1.5 %copy-start.11 = (bf16[64,2048]{1,0:T(8,128)(2,1)}, bf16[64,2048]{1,0:T(8,128)(2,1)S(1)}, u32[]{:S(2)}) copy-start(bf16[64,2048]{1,0:T(8,128)(2,1)S(1)} %collective-permute-done.8.refs_9_) | copy-start | bytes 786436
  45.1 1.4 %collective-permute-start.19 = (bf16[32,2048]{1,0:T(8,128)(2,1)S(1)}, bf16[32,2048]{1,0:T(8,128)(2,1)S(1)}, u32[]{:S(2)}, u32[]{:S(2)}) collective-permute-start(bf16[32,2048]{1,0:T(8,128)(2,1)S(1)} %collective-permute-done.18.refs_16_), channel_id=1, source_target_pairs={{0,2},{2,0},{8,10},{10,8},{16,18},{18,16},{24,26},{26,24},{28,30},... | collective-permute-start | bytes 393224 | tf_op jit(solution)/shard_map/ppermute | solution.py:352
  45.5 1.1 %copy-start.12 = (bf16[64,2048]{1,0:T(8,128)(2,1)}, bf16[64,2048]{1,0:T(8,128)(2,1)S(1)}, u32[]{:S(2)}) copy-start(bf16[64,2048]{1,0:T(8,128)(2,1)S(1)} %collective-permute-done.6.refs_7_) | copy-start | bytes 786436
  73.7 28.0 %collective-permute-start.22 = (bf16[128,2048]{1,0:T(8,128)(2,1)S(1)}, bf16[128,2048]{1,0:T(8,128)(2,1)S(1)}, u32[]{:S(2)}, u32[]{:S(2)}) collective-permute-start(bf16[128,2048]{1,0:T(8,128)(2,1)S(1)} %get-tuple-element.29), channel_id=1, source_target_pairs={{0,1},{1,0},{2,3},{3,2},{4,5},{5,4},{6,7},{7,6},{8,9},{9,8},{10,11... | collective-permute-start | bytes 1572872 | tf_op jit(solution)/shard_map/ppermute | solution.py:395
  87.5 14.2 %collective-permute-start.23 = (bf16[64,2048]{1,0:T(8,128)(2,1)S(1)}, bf16[64,2048]{1,0:T(8,128)(2,1)S(1)}, u32[]{:S(2)}, u32[]{:S(2)}) collective-permute-start(bf16[64,2048]{1,0:T(8,128)(2,1)S(1)} %query_type.2), channel_id=1, source_target_pairs={{0,1},{1,0},{2,3},{3,2},{4,5},{5,4},{6,7},{7,6},{8,9},{9,8},{10,11... | collective-permute-start | bytes 786440 | tf_op jit(solution)/shard_map/ppermute | solution.py:395
  100.1 8.0 %collective-permute-start.24 = (bf16[64,2048]{1,0:T(8,128)(2,1)S(1)}, bf16[64,2048]{1,0:T(8,128)(2,1)S(1)}, u32[]{:S(2)}, u32[]{:S(2)}) collective-permute-start(bf16[64,2048]{1,0:T(8,128)(2,1)S(1)} %query_type.3), channel_id=1, source_target_pairs={{0,1},{1,0},{2,3},{3,2},{4,5},{5,4},{6,7},{7,6},{8,9},{9,8},{10,11... | collective-permute-start | bytes 786440 | tf_op jit(solution)/shard_map/ppermute | solution.py:395
